TPU v7x, 256 devices: a whole 4x4x8 slice. The times are simulated.
256 devices in a mesh: dp: 16 (over z_lo, x, core), row: 4 (over y), col: 4 (over z_hi).
Axes of the slice: x: 4, y: 4, z: 8 (z_hi: 4, z_lo: 2; z = z_hi * 2 + z_lo), core: 2. Of those that a mesh axis runs over, the one named last changes fastest.
Arguments:
- tokens: bfloat16 [2048, 4096], P(('dp', 'col'), 'row'), may hold values from -6 to 6
- up_weight: bfloat16 [4096, 8192], P('row', 'col'), may hold values from -0.09375 to 0.09375
- up_bias: float32 [8192], P('col'), may hold values from -3 to 3
- down_weight: bfloat16 [8192, 4096], P('col', 'row'), may hold values from -0.0625 to 0.0625
- out_grad: bfloat16 [2048, 4096], P(('dp', 'col'), 'row'), may hold values from -6 to 6
- bucket_lengths: int32 [64], P(('dp', 'col')), may hold values from 1 to 32, as said below
Outputs:
- input_grad: bfloat16 [2048, 4096], P(('dp', 'col'), 'row')
- up_weight_grad: float32 [4096, 4, 2048], P('row', 'col', 'dp')
- up_bias_grad: float32 [4, 2048], P('col', 'dp')
- down_weight_grad: float32 [4, 2048, 4096], P('col', 'dp', 'row')
Inputs may be any that keep to these rules, and one draw needn't show every extreme that they name: `bucket_lengths`: some block is full.
All inputs are finite; a program needn't handle non-finite values.
Results may differ from a plain program's by a relative error of at most 0.0055.
Values may be sent and summed in bfloat16 or wider, within the bound.
No kernel may reach another device: no remote copies, remote signals or barrier semaphores. Data moves between devices by JAX's collectives and lax.ppermute only.
A program may use at most 128 MiB of HBM per device.

v0:
```python
import math

import jax
import jax.numpy as jnp
from jax import lax
from jax.sharding import PartitionSpec as P

coef = math.sqrt(2.0 / math.pi)


def gelu_pair(pre):
    inner = coef * (pre + 0.044715 * pre * pre * pre)
    tanh_val = jnp.tanh(inner)
    value = 0.5 * pre * (1.0 + tanh_val)
    slope = 0.5 * (1.0 + tanh_val) + 0.5 * pre * (1.0 - tanh_val * tanh_val) * coef * (
        1.0 + 3.0 * 0.044715 * pre * pre
    )
    return (value, slope)


def contract_rows(left, right):
    return lax.dot_general(
        left, right, (((0,), (0,)), ((), ())), preferred_element_type=jnp.float32
    )


def contract_cols(left, right):
    return lax.dot_general(
        left, right, (((1,), (1,)), ((), ())), preferred_element_type=jnp.float32
    )


def local(tokens, up_weight, up_bias, down_weight, out_grad, bucket_lengths):
    local_rows = out_grad.shape[0]
    blocks = bucket_lengths.shape[0]
    block_rows = local_rows // blocks
    position = jnp.arange(local_rows, dtype=jnp.int32)
    limits = jnp.repeat(bucket_lengths, block_rows, total_repeat_length=local_rows)
    live = position % block_rows < limits
    masked = jnp.where(live[:, None], out_grad, jnp.zeros_like(out_grad))
    feats, grads = (
        lax.all_gather(tokens, "col", axis=0, tiled=True),
        lax.all_gather(masked, "col", axis=0, tiled=True),
    )
    down_grad = None
    pre = lax.psum(jnp.dot(feats, up_weight, preferred_element_type=jnp.float32), "row")
    value, slope = gelu_pair(pre + up_bias[None, :])
    act_all = value.astype(jnp.bfloat16)
    act_grad = lax.psum(contract_cols(grads, down_weight), "row")
    grad_all = (act_grad * slope).astype(jnp.bfloat16)
    up_term = contract_rows(feats, grad_all)
    bias_term = jnp.sum(grad_all.astype(jnp.float32), axis=0)[None, :]
    input_grad = lax.psum_scatter(
        contract_cols(
            lax.slice_in_dim(grad_all, 0, local_rows * lax.axis_size("col"), axis=0), up_weight
        ),
        "col",
        scatter_dimension=0,
        tiled=True,
    ).astype(jnp.bfloat16)
    up_grad, bias_grad = (
        lax.psum_scatter(up_term, "dp", scatter_dimension=1, tiled=True),
        lax.psum_scatter(bias_term, "dp", scatter_dimension=1, tiled=True),
    )
    down_grad = lax.psum_scatter(
        contract_rows(act_all, grads), "dp", scatter_dimension=0, tiled=True
    )
    narrow = up_grad.shape[1]
    return (
        input_grad,
        up_grad.reshape(up_grad.shape[0], 1, narrow),
        bias_grad.reshape(1, narrow),
        down_grad.reshape(1, narrow, down_grad.shape[1]),
    )


def solution(mesh):
    return jax.shard_map(
        local,
        mesh=mesh,
        in_specs=(
            P(("dp", "col"), "row"),
            P("row", "col"),
            P("col"),
            P("col", "row"),
            P(("dp", "col"), "row"),
            P(("dp", "col")),
        ),
        out_specs=(
            P(("dp", "col"), "row"),
            P("row", "col", "dp"),
            P("col", "dp"),
            P("col", "dp", "row"),
        ),
        check_vma=False,
    )
```

profile of v0, /device:TPU:1, one launch (start us, length us, event | category | flops | bytes accessed | tf_op | source)
XLA Modules:
  0.0 367.5 jit_solution(2555846594307156980)
XLA Ops:
  7.2 0.0 all-reduce.3.cloned.1.call-start
  8.0 1.1 broadcast_select_fusion
  9.1 16.3 %all_gather.6 = bf16[128,1024]{1,0:T(8,128)(2,1)S(1)} all-gather(bf16[32,1024]{1,0:T(8,128)(2,1)S(1)} %broadcast_select_fusion), channel_id=1, replica_groups=mesh['dp'=16,'row'=4,'col'=4] {'col'}, dimensions={0}, use_global_device_ids=true | all-gather | bytes 327680 | tf_op jit(solution)/shard_map/all_gather | solution.py:43
  25.4 11.4 %all_gather.7 = bf16[128,1024]{1,0:T(8,128)(2,1)S(1)} all-gather(bf16[32,1024]{1,0:T(8,128)(2,1)} %param.10), channel_id=1, replica_groups=mesh['dp'=16,'row'=4,'col'=4] {'col'}, dimensions={0}, use_global_device_ids=true | all-gather | bytes 327680 | tf_op jit(solution)/shard_map/all_gather | solution.py:42
  36.8 3.9 %fusion.20 = f32[128,2048]{1,0:T(8,128)} fusion(bf16[128,1024]{1,0:T(8,128)(2,1)S(1)} %all_gather.7, bf16[1024,2048]{1,0:T(8,128)(2,1)} %param.11), kind=kOutput, calls=%fused_computation.26 | convolution fusion | flops 536870912 | bytes 5505024 | tf_op jit(solution)/shard_map/dot_general | solution.py:46
  40.7 2.5 fusion.19
  43.3 0.0 reduce-scatter.13.cloned.1.call-start
  43.4 68.8 %all-reduce.3.cloned.1.call-done = (f32[128,2048]{1,0:T(8,128)}, f32[128,2048]{1,0:T(8,128)}) async-done(((f32[128,2048]{1,0:T(8,128)}, f32[128,2048]{1,0:T(8,128)}), (f32[128,2048]{1,0:T(8,128)}, f32[128,2048]{1,0:T(8,128)})) %all-reduce.3.cloned.1.call-update) | async-done | bytes 2097168 | tf_op jit(solution)/shard_map/psum | solution.py:49
  112.1 2.3 convert_reduce_fusion
  114.4 1.3 copy.12
  115.8 0.0 reduce-scatter.7.cloned.1.call-start
  115.8 4.5 %fusion.21 = f32[128,1024]{1,0:T(8,128)} fusion(bf16[128,2048]{1,0:T(8,128)(2,1)S(1)} %get-tuple-element.39, bf16[1024,2048]{1,0:T(8,128)(2,1)} %param.11), kind=kOutput, calls=%fused_computation.27 | convolution fusion | flops 536870912 | bytes 5242880 | tf_op jit(solution)/shard_map/dot_general | solution.py:28
  120.3 0.0 reduce-scatter.9.cloned.1.call-start
  120.4 4.5 %convolution_bitcast_fusion = f32[1024,2048]{0,1:T(8,128)} fusion(bf16[128,2048]{1,0:T(8,128)(2,1)S(1)} %get-tuple-element.39, bf16[128,1024]{1,0:T(8,128)(2,1)S(1)} %all_gather.7), kind=kOutput, calls=%fused_computation | convolution fusion | flops 536870912 | bytes 9175040 | tf_op jit(solution)/shard_map/dot_general | solution.py:22
  124.9 0.0 reduce-scatter.11.cloned.1.call-start
  125.0 1.1 copy-done
  126.1 4.5 %fusion.7 = f32[2048,1024]{1,0:T(8,128)} fusion(bf16[128,1024]{1,0:T(8,128)(2,1)S(1)} %all_gather.6, f32[128,2048]{1,0:T(8,128)S(1)} %copy-done, f32[2048]{0:T(1024)S(1)} %copy-done.2), kind=kOutput, calls=%fused_computation.12 | convolution fusion | flops 539492352 | bytes 9707520 | tf_op jit(solution)/shard_map/dot_general | solution.py:22
  130.7 45.7 %reduce-scatter.13.cloned.1.call-done = f32[128,1]{1,0:T(8,128)} async-done(((f32[2048,1]{1,0:T(8,128)}), f32[128,1]{1,0:T(8,128)}) %reduce-scatter.13.cloned.1.call-update) | async-done | bytes 528
  176.3 1.4 copy.13
  177.8 29.9 %reduce-scatter.7.cloned.1.call-done = f32[32,1024]{1,0:T(8,128)} async-done(((f32[128,1024]{1,0:T(8,128)}), f32[32,1024]{1,0:T(8,128)}) %reduce-scatter.7.cloned.1.call-update) | async-done | bytes 131088 | tf_op jit(solution)/shard_map/reduce_scatter | solution.py:53
  207.7 1.5 convert_element_type.13
  209.2 73.8 %reduce-scatter.9.cloned.1.call-done = f32[1024,128]{0,1:T(8,128)} async-done(((f32[1024,2048]{0,1:T(8,128)}), f32[1024,128]{0,1:T(8,128)}) %reduce-scatter.9.cloned.1.call-update) | async-done | bytes 524304 | tf_op jit(solution)/shard_map/reduce_scatter | solution.py:62
  283.0 1.9 copy.11
  284.9 76.1 %reduce-scatter.11.cloned.1.call-done = f32[128,1024]{1,0:T(8,128)} async-done(((f32[2048,1024]{1,0:T(8,128)}), f32[128,1024]{1,0:T(8,128)}) %reduce-scatter.11.cloned.1.call-update) | async-done | bytes 524304 | tf_op jit(solution)/shard_map/reduce_scatter | solution.py:65
  (11 shorter events, 0.1 us)
Async XLA Ops:
  7.2 104.9 %all-reduce.3.cloned.1.call-start = ((), (), s32[]{:S(2)}) async-start(), calls=%async_computation.8 | async-start | bytes 4194304 | tf_op jit(solution)/shard_map/psum | solution.py:49
  7.2 33.5 %copy-start.1 = (bf16[2048,1024]{1,0:T(8,128)(2,1)S(1)}, bf16[2048,1024]{1,0:T(8,128)(2,1)}, u32[]{:S(2)}) copy-start(bf16[2048,1024]{1,0:T(8,128)(2,1)} %param.13) | copy-start | bytes 12582916
  40.7 71.4 %copy-start.2 = (f32[2048]{0:T(1024)S(1)}, f32[2048]{0:T(1024)}, u32[]{:S(2)}) copy-start(f32[2048]{0:T(1024)} %param.12) | copy-start | bytes 24580
  43.3 133.0 %reduce-scatter.13.cloned.1.call-start = ((), (), s32[]{:S(2)}) async-start(), calls=%async_computation.7 | async-start | bytes 1114112
  115.8 91.9 %reduce-scatter.7.cloned.1.call-start = ((), (), s32[]{:S(2)}) async-start(), calls=%async_computation.4 | async-start | bytes 655360 | tf_op jit(solution)/shard_map/reduce_scatter | solution.py:53
  120.3 162.6 %reduce-scatter.9.cloned.1.call-start = ((), (), s32[]{:S(2)}) async-start(), calls=%async_computation.5 | async-start | bytes 8912896 | tf_op jit(solution)/shard_map/reduce_scatter | solution.py:62
  124.9 1.2 copy-start
  124.9 236.1 %reduce-scatter.11.cloned.1.call-start = ((), (), s32[]{:S(2)}) async-start(), calls=%async_computation.6 | async-start | bytes 8912896 | tf_op jit(solution)/shard_map/reduce_scatter | solution.py:65
Sparse Core Ops, SparseCore 0:
  43.4 68.6 all-reduce.2
  115.9 60.3 reduce-scatter.12
  179.4 28.1 reduce-scatter.6
  210.1 72.8 reduce-scatter.8
  285.9 75.0 reduce-scatter.10
where the time goes:
time: 371 us; the launch traced here: 368 us
  waiting for transfers between devices  294 us (79%)
  blocking collectives  27.7 us (7%)
  matrix products  20 us (5%)
  between operations  14.6 us (4%)
  local copies, waits for them, and re-layouts  5.86 us (2%)
  other arithmetic  4.93 us (1%)
    reduce_scatter x1, waiting for transfers between devices, local(): lax.psum_scatter(contract_rows(act_all, grads), 'dp', scatter_dimension=0...  76.1 us
    reduce_scatter x1, waiting for transfers between devices, local(): lax.psum_scatter(up_term, 'dp', scatter_dimension=1, tiled=True)  73.8 us
    psum x1, waiting for transfers between devices, local(): act_grad = lax.psum(contract_cols(grads, down_weight), 'row')  68.8 us
    unnamed x6, waiting for transfers between devices  45.7 us
    reduce_scatter x1, waiting for transfers between devices, local(): lax.psum_scatter(contract_cols(lax.slice_in_dim(grad_all, 0, local_rows *...  29.9 us
    all_gather x1, blocking collectives, local(): lax.all_gather(masked, 'col', axis=0, tiled=True)  16.3 us
    all_gather x1, blocking collectives, local(): lax.all_gather(tokens, 'col', axis=0, tiled=True)  11.4 us
    dot_general x2, matrix products, contract_rows(): lax.dot_general(left, right, (((0,), (0,)), ((), ())), preferred_element_...  9.04 us
  transfers between devices with their start and end apart: 5, of which 5 were waited for; matrix products, arithmetic and copies ran while one was open for 5% of the time, Pallas kernels for 0%

commit v1 on v0

v1 whole, which is shorter than its diff:
```python
import math

import jax
import jax.numpy as jnp
from jax import lax
from jax.sharding import PartitionSpec as P

coef = math.sqrt(2.0 / math.pi)


def gelu_pair(pre):
    inner = coef * (pre + 0.044715 * pre * pre * pre)
    tanh_val = jnp.tanh(inner)
    value = 0.5 * pre * (1.0 + tanh_val)
    slope = 0.5 * (1.0 + tanh_val) + 0.5 * pre * (1.0 - tanh_val * tanh_val) * coef * (
        1.0 + 3.0 * 0.044715 * pre * pre
    )
    return (value, slope)


def dot(left, right, dims):
    return lax.dot_general(left, right, (dims, ((), ())), preferred_element_type=jnp.float32)


def sum_parts(parts):
    return jnp.sum(parts.astype(jnp.float32), axis=0)


def spread(array, axis):
    count = lax.axis_size(axis)
    return lax.all_to_all(jnp.broadcast_to(array[None], (count, *array.shape)), axis, 0, 0)


def local(tokens, up_weight, up_bias, down_weight, out_grad, bucket_lengths):
    rows, width = out_grad.shape
    hidden = up_weight.shape[1]
    n_dp, n_row, n_col = lax.axis_size("dp"), lax.axis_size("row"), lax.axis_size("col")
    blocks = bucket_lengths.shape[0]
    block_rows = rows // blocks
    position = jnp.arange(rows, dtype=jnp.int32)
    limits = jnp.repeat(bucket_lengths, block_rows, total_repeat_length=rows)
    live = position % block_rows < limits
    masked = jnp.where(live[:, None], out_grad, jnp.zeros_like(out_grad))
    both = jnp.concatenate([tokens, masked], axis=1)
    group = lax.all_gather(both, "col", axis=0, tiled=True)
    group_all = lax.all_gather(group, "dp", axis=0, tiled=True)

    pre_part = dot(group[:, :width], up_weight, ((1,), (0,))).astype(jnp.bfloat16)
    act_grad_part = dot(group[:, width:], down_weight, ((1,), (1,))).astype(jnp.bfloat16)
    parts = jnp.concatenate(
        [pre_part.reshape(n_row, rows, hidden), act_grad_part.reshape(n_row, rows, hidden)], axis=1
    )
    sums = sum_parts(lax.all_to_all(parts, "row", 0, 0))
    value, slope = gelu_pair(sums[:rows] + up_bias[None, :])
    act = value.astype(jnp.bfloat16)
    pre_grad = (sums[rows:] * slope).astype(jnp.bfloat16)

    narrow = hidden // n_dp
    pair = jnp.stack([act, pre_grad]).reshape(2, rows, n_dp, narrow).transpose(2, 0, 1, 3)
    pair = lax.all_to_all(pair, "dp", 0, 0)
    pair_all = spread(pair, "row")
    pair_all = pair_all.transpose(2, 1, 0, 3, 4).reshape(2, n_dp * n_row * rows, narrow)
    act_all, pre_grad_all = pair_all[0], pair_all[1]

    pre_grad_group = spread(pre_grad, "row").reshape(n_row * rows, hidden)
    input_part = dot(pre_grad_group, up_weight, ((1,), (1,))).astype(jnp.bfloat16)
    input_grad = sum_parts(
        lax.all_to_all(input_part.reshape(n_col, rows, width), "col", 0, 0)
    ).astype(jnp.bfloat16)

    up_grad = dot(group_all[:, :width], pre_grad_all, ((0,), (0,)))
    down_grad = dot(act_all, group_all[:, width:], ((0,), (0,)))
    bias_grad = jnp.sum(pre_grad_all.astype(jnp.float32), axis=0)
    return (
        input_grad,
        up_grad.reshape(width, 1, narrow),
        bias_grad.reshape(1, narrow),
        down_grad.reshape(1, narrow, width),
    )


def solution(mesh):
    return jax.shard_map(
        local,
        mesh=mesh,
        in_specs=(
            P(("dp", "col"), "row"),
            P("row", "col"),
            P("col"),
            P("col", "row"),
            P(("dp", "col"), "row"),
            P(("dp", "col")),
        ),
        out_specs=(
            P(("dp", "col"), "row"),
            P("row", "col", "dp"),
            P("col", "dp"),
            P("col", "dp", "row"),
        ),
        check_vma=False,
    )
```

time: 371 us -> 132 us (0.36)
  the two profiles are of different devices: /device:TPU:1 before, /device:TPU:6 now
where the time goes in v1:
time: 132 us
  waiting for transfers between devices  39 us (30%)
  blocking collectives  37.1 us (28%)
  matrix products  17.1 us (13%)
  starting transfers between devices  16.6 us (13%)
  between operations  14.8 us (11%)
  other arithmetic  3.71 us (3%)
  local copies, waits for them, and re-layouts  3.15 us (2%)
    all_to_all x2, waiting for transfers between devices, spread(): lax.all_to_all(jnp.broadcast_to(array[None], (count, *array.shape)), axis...  22 us
    all_gather x1, blocking collectives, local(): group = lax.all_gather(both, 'col', axis=0, tiled=True)  20.7 us
    dot_general x5, matrix products, dot(): lax.dot_general(left, right, (dims, ((), ())), preferred_element_type=jnp...  17.1 us
    all_to_all x1, blocking collectives, local(): sums = sum_parts(lax.all_to_all(parts, 'row', 0, 0))  16.4 us
    all_to_all x1, waiting for transfers between devices, local(): lax.all_to_all(input_part.reshape(n_col, rows, width), 'col', 0, 0)  13.4 us
    all_to_all x2, starting transfers between devices, spread(): lax.all_to_all(jnp.broadcast_to(array[None], (count, *array.shape)), axis...  7.06 us
    all_to_all x1, starting transfers between devices, local(): pair = lax.all_to_all(pair, 'dp', 0, 0)  4.78 us
    all_to_all x1, starting transfers between devices, local(): lax.all_to_all(input_part.reshape(n_col, rows, width), 'col', 0, 0)  4.76 us
  transfers between devices with their start and end apart: 5, of which 4 were waited for; matrix products, arithmetic and copies ran while one was open for 11% of the time, Pallas kernels for 0%

profile of v1, /device:TPU:6, one launch (start us, length us, event | category | flops | bytes accessed | tf_op | source)
XLA Modules:
  0.0 131.6 jit_solution(7724745762595005737)
XLA Ops:
  7.9 0.9 broadcast_select_fusion
  8.8 0.8 pad_maximum_fusion.1
  9.6 20.7 %all_gather.6 = bf16[128,2048]{1,0:T(8,128)(2,1)} all-gather(bf16[32,2048]{1,0:T(8,128)(2,1)S(1)} %pad_maximum_fusion.1), channel_id=1, replica_groups=mesh['dp'=16,'row'=4,'col'=4] {'col'}, dimensions={0}, use_global_device_ids=true | all-gather | bytes 655360 | tf_op jit(solution)/shard_map/all_gather | solution.py:45
  30.4 3.9 %convolution_convert_fusion = bf16[128,2048]{1,0:T(8,128)(2,1)S(1)} fusion(bf16[2048,1024]{1,0:T(8,128)(2,1)} %param.13, bf16[128,2048]{1,0:T(8,128)(2,1)} %all_gather.6), kind=kOutput, calls=%fused_computation.4 | convolution fusion | flops 537133056 | bytes 4980736 | tf_op jit(solution)/shard_map/dot_general | solution.py:22
  34.3 0.7 convolution_convert_fusion.1
  35.2 16.4 %all_to_all.25 = bf16[4,64,2048]{2,1,0:T(8,128)(2,1)S(1)} all-to-all(bf16[4,64,2048]{2,1,0:T(8,128)(2,1)S(1)} %pad_maximum_fusion), channel_id=1, replica_groups=mesh['dp'=16,'row'=4,'col'=4] {'row'}, dimensions={0} | all-to-all | bytes 2097152 | tf_op jit(solution)/shard_map/all_to_all | solution.py:53
  51.6 0.2 convert_reduce_fusion
  51.8 0.2 fusion.16
  52.0 0.8 broadcast_in_dim.20
  52.8 3.5 %all-to-all-start.1 = ((bf16[4,32,2048]{2,1,0:T(8,128)(2,1)}), bf16[4,32,2048]{2,1,0:T(8,128)(2,1)S(1)}, u32[]{:S(2)}, u32[]{:S(2)}) async-start(bf16[4,32,2048]{2,1,0:T(8,128)(2,1)} %broadcast_in_dim.20), calls=%async_computation.1 | async-start | bytes 1048576 | tf_op jit(solution)/shard_map/all_to_all | solution.py:31
  56.4 0.8 copy.15
  57.2 7.2 %all-to-all-done.1 = bf16[4,32,2048]{2,1,0:T(8,128)(2,1)S(1)} async-done(((bf16[4,32,2048]{2,1,0:T(8,128)(2,1)}), bf16[4,32,2048]{2,1,0:T(8,128)(2,1)S(1)}, u32[]{:S(2)}, u32[]{:S(2)}) %all-to-all-start.1) | async-done | bytes 524320 | tf_op jit(solution)/shard_map/all_to_all | solution.py:31
  64.4 4.8 %all-to-all-start.3 = ((bf16[16,2,32,128]{3,2,1,0:T(8,128)(2,1)}), bf16[16,2,32,128]{3,2,1,0:T(8,128)(2,1)S(1)}, u32[]{:S(2)}, u32[]{:S(2)}) async-start(bf16[16,2,32,128]{3,2,1,0:T(8,128)(2,1)} %copy.15), calls=%async_computation.3 | async-start | bytes 524288 | tf_op jit(solution)/shard_map/all_to_all | solution.py:60
  69.2 4.5 %convolution_convert_fusion.2 = bf16[128,1024]{1,0:T(8,128)(2,1)} fusion(bf16[128,2048]{1,0:T(8,128)(2,1)S(1)} %bitcast.34, bf16[1024,2048]{1,0:T(8,128)(2,1)} %param.11), kind=kOutput, calls=%fused_computation.8 | convolution fusion | flops 537001984 | bytes 4980736 | tf_op jit(solution)/shard_map/dot_general | solution.py:22
  73.7 3.6 %all-to-all-done.3 = bf16[16,2,32,128]{3,2,1,0:T(8,128)(2,1)S(1)} async-done(((bf16[16,2,32,128]{3,2,1,0:T(8,128)(2,1)}), bf16[16,2,32,128]{3,2,1,0:T(8,128)(2,1)S(1)}, u32[]{:S(2)}, u32[]{:S(2)}) %all-to-all-start.3) | async-done | bytes 262176 | tf_op jit(solution)/shard_map/all_to_all | solution.py:60
  77.2 4.8 %all-to-all-start.2 = ((bf16[4,32,1024]{2,1,0:T(8,128)(2,1)}), bf16[4,32,1024]{2,1,0:T(8,128)(2,1)S(1)}, u32[]{:S(2)}, u32[]{:S(2)}) async-start(bf16[4,32,1024]{2,1,0:T(8,128)(2,1)} %bitcast.4), calls=%async_computation.2 | async-start | bytes 524288 | tf_op jit(solution)/shard_map/all_to_all | solution.py:68
  82.0 13.4 %all-to-all-done.2 = bf16[4,32,1024]{2,1,0:T(8,128)(2,1)S(1)} async-done(((bf16[4,32,1024]{2,1,0:T(8,128)(2,1)}), bf16[4,32,1024]{2,1,0:T(8,128)(2,1)S(1)}, u32[]{:S(2)}, u32[]{:S(2)}) %all-to-all-start.2) | async-done | bytes 262176 | tf_op jit(solution)/shard_map/all_to_all | solution.py:68
  95.4 1.2 broadcast_in_dim.21
  96.7 3.6 %all-to-all-start.4 = ((bf16[4,16,2,32,128]{4,3,1,2,0:T(8,128)(2,1)}), bf16[4,16,2,32,128]{4,3,1,2,0:T(8,128)(2,1)S(1)}, u32[]{:S(2)}, u32[]{:S(2)}) async-start(bf16[4,16,2,32,128]{4,3,1,2,0:T(8,128)(2,1)} %broadcast_in_dim.21), calls=%async_computation.4 | async-start | bytes 2097152 | tf_op jit(solution)/shard_map/all_to_all | solution.py:31
  100.2 0.7 reduce_sum.31
  100.9 14.8 %all-to-all-done.4 = bf16[4,16,2,32,128]{4,3,1,2,0:T(8,128)(2,1)S(1)} async-done(((bf16[4,16,2,32,128]{4,3,1,2,0:T(8,128)(2,1)}), bf16[4,16,2,32,128]{4,3,1,2,0:T(8,128)(2,1)S(1)}, u32[]{:S(2)}, u32[]{:S(2)}) %all-to-all-start.4) | async-done | bytes 1048608 | tf_op jit(solution)/shard_map/all_to_all | solution.py:31
  115.9 0.8 convert_reduce_fusion.1
  116.8 3.7 %fusion.4 = f32[1,128,1024]{2,1,0:T(8,128)} fusion(bf16[2048,128]{1,0:T(8,128)(2,1)S(1)} %bitcast.35, bf16[2048,2048]{1,0:T(8,128)(2,1)} %all-gather.2.cloned.1.call-done), kind=kOutput, calls=%fused_computation.7 | convolution fusion | flops 536870912 | bytes 5242880 | tf_op jit(solution)/shard_map/dot_general | solution.py:22
  120.5 4.3 %fusion.2 = f32[1024,128]{1,0:T(8,128)} fusion(bf16[2048,128]{1,0:T(8,128)(2,1)S(1)} %bitcast.41, bf16[2048,2048]{1,0:T(8,128)(2,1)} %all-gather.2.cloned.1.call-done), kind=kOutput, calls=%fused_computation.2 | convolution fusion | flops 536870912 | bytes 5242880 | tf_op jit(solution)/shard_map/dot_general | solution.py:22
  (17 shorter events, 0.5 us)
Async XLA Ops:
  7.2 109.6 %all-gather.2.cloned.1.call-start = ((), (), s32[]{:S(2)}) async-start(), calls=%async_computation.5 | async-start | bytes 8912896 | tf_op jit(solution)/shard_map/all_gather | solution.py:46
  30.3 4.0 %copy-start.1 = (bf16[128,2048]{1,0:T(8,128)(2,1)S(1)}, bf16[128,2048]{1,0:T(8,128)(2,1)}, u32[]{:S(2)}) copy-start(bf16[128,2048]{1,0:T(8,128)(2,1)} %all_gather.6) | copy-start | bytes 1572868
  30.4 4.0 %copy-start = (bf16[1024,2048]{1,0:T(8,128)(2,1)S(1)}, bf16[1024,2048]{1,0:T(8,128)(2,1)}, u32[]{:S(2)}) copy-start(bf16[1024,2048]{1,0:T(8,128)(2,1)} %param.11) | copy-start | bytes 12582916
  34.3 17.4 %copy-start.2 = (f32[2048]{0:T(1024)S(1)}, f32[2048]{0:T(1024)}, u32[]{:S(2)}) copy-start(f32[2048]{0:T(1024)} %param.12) | copy-start | bytes 24580
  52.8 11.5 %all-to-all-start.1 = ((bf16[4,32,2048]{2,1,0:T(8,128)(2,1)}), bf16[4,32,2048]{2,1,0:T(8,128)(2,1)S(1)}, u32[]{:S(2)}, u32[]{:S(2)}) async-start(bf16[4,32,2048]{2,1,0:T(8,128)(2,1)} %broadcast_in_dim.20), calls=%async_computation.1 | async-start | bytes 1048576 | tf_op jit(solution)/shard_map/all_to_all | solution.py:31
  64.4 12.9 %all-to-all-start.3 = ((bf16[16,2,32,128]{3,2,1,0:T(8,128)(2,1)}), bf16[16,2,32,128]{3,2,1,0:T(8,128)(2,1)S(1)}, u32[]{:S(2)}, u32[]{:S(2)}) async-start(bf16[16,2,32,128]{3,2,1,0:T(8,128)(2,1)} %copy.15), calls=%async_computation.3 | async-start | bytes 524288 | tf_op jit(solution)/shard_map/all_to_all | solution.py:60
  77.2 18.2 %all-to-all-start.2 = ((bf16[4,32,1024]{2,1,0:T(8,128)(2,1)}), bf16[4,32,1024]{2,1,0:T(8,128)(2,1)S(1)}, u32[]{:S(2)}, u32[]{:S(2)}) async-start(bf16[4,32,1024]{2,1,0:T(8,128)(2,1)} %bitcast.4), calls=%async_computation.2 | async-start | bytes 524288 | tf_op jit(solution)/shard_map/all_to_all | solution.py:68
  96.7 19.0 %all-to-all-start.4 = ((bf16[4,16,2,32,128]{4,3,1,2,0:T(8,128)(2,1)}), bf16[4,16,2,32,128]{4,3,1,2,0:T(8,128)(2,1)S(1)}, u32[]{:S(2)}, u32[]{:S(2)}) async-start(bf16[4,16,2,32,128]{4,3,1,2,0:T(8,128)(2,1)} %broadcast_in_dim.21), calls=%async_computation.4 | async-start | bytes 2097152 | tf_op jit(solution)/shard_map/all_to_all | solution.py:31
Sparse Core Ops, SparseCore 0:
  30.5 60.4 all-gather.1

commit v2 on v1

v2 whole, which is shorter than its diff:
```python
import math

import jax
import jax.numpy as jnp
from jax import lax
from jax.experimental import pallas as pl
from jax.experimental.pallas import tpu as pltpu
from jax.sharding import PartitionSpec as P

coef = math.sqrt(2.0 / math.pi)
ZL, NX, NC = 2, 4, 2
PEERS = ZL * NX
SIDE = 4
MASK, GELU, INPUT, WEIGHT = 64, 32, 64, 64
VMEM = pl.BlockSpec(memory_space=pltpu.VMEM)
SMEM = pl.BlockSpec(memory_space=pltpu.SMEM)
bf16, f32 = jnp.bfloat16, jnp.float32


def gelu_pair(pre):
    inner = coef * (pre + 0.044715 * pre * pre * pre)
    tanh_val = jnp.tanh(inner)
    value = 0.5 * pre * (1.0 + tanh_val)
    slope = 0.5 * (1.0 + tanh_val) + 0.5 * pre * (1.0 - tanh_val * tanh_val) * coef * (
        1.0 + 3.0 * 0.044715 * pre * pre
    )
    return (value, slope)


def dot(left, right, dims):
    return lax.dot_general(left, right, (dims, ((), ())), preferred_element_type=f32)


def shape(dims, kind):
    return jax.ShapeDtypeStruct(dims, kind)


def call(kernel, outs, scratch, cost, *args, smem=0, tail=0, name=None):
    return pl.pallas_call(
        kernel,
        out_shape=outs,
        in_specs=[SMEM] * smem + [VMEM] * (len(args) - smem),
        out_specs=(VMEM,) * (len(outs) - tail) + (SMEM,) * tail,
        scratch_shapes=scratch,
        compiler_params=pltpu.CompilerParams(vmem_limit_bytes=24 << 20),
        cost_estimate=pl.CostEstimate(flops=cost[0], bytes_accessed=cost[1], transcendentals=0),
        name=name,
    )(*args)


def shift(array, axis, by):
    count = lax.axis_size(axis)
    return lax.ppermute(array, axis, [(i, (i + by) % count) for i in range(count)])


def move(array, step):
    pairs = []
    for z in range(ZL):
        for x in range(NX):
            for c in range(NC):
                tz, tx, tc = step(z, x, c)
                pairs.append(((z * NX + x) * NC + c, (tz * NX + tx) * NC + tc))
    return lax.ppermute(array, "dp", pairs)


def shift_x(array, by):
    return move(array, lambda z, x, c: (z, (x + by) % NX, c))


def flip_z(array):
    return move(array, lambda z, x, c: (1 - z, x, c))


def flip_core(array):
    return move(array, lambda z, x, c: (z, x, 1 - c))


def mask_kernel(lengths, tokens, out_grad, both):
    rows, width = tokens.shape
    live = lax.broadcasted_iota(jnp.int32, (rows, width), 0) < lengths[0]
    both[:, :width] = tokens[...]
    both[:, width:] = jnp.where(live, out_grad[...], jnp.zeros_like(out_grad))


def near_kernel(place, up, down, same):
    for i in range(4):
        same[i] = place[i]


def first_kernel(place, b0, b1, b2, b3, up, down, group, keep, s1, s2, s3, parts):
    rows, both = b0.shape
    width, hidden = up.shape
    row = place[0]
    for k, block in enumerate((b0, b1, b2, b3)):
        group[k * rows : (k + 1) * rows, :] = block[...]
    tile = 512
    for t in range(hidden // tile):
        at = slice(t * tile, (t + 1) * tile)
        pre = dot(group[:, :width], up[:, at], ((1,), (0,)))
        act = dot(group[:, width:], down[at, :], ((1,), (1,)))
        for k in range(SIDE):
            own = slice(k * rows, (k + 1) * rows)
            parts[k, :rows, at] = pre[own]
            parts[k, rows:, at] = act[own]
    keep[...] = parts[row]
    for k, send in ((1, s1), (2, s2), (3, s3)):
        send[...] = parts[lax.rem(row + k, SIDE)].astype(bf16)


def gelu_kernel(keep, r1, r2, r3, bias, pair, pre_grad):
    rows = keep.shape[0] // 2
    wide = pair.shape[2]
    for p in range(PEERS):
        at = slice(p * wide, (p + 1) * wide)
        total = keep[:, at] + r1[:, at].astype(f32) + r2[:, at].astype(f32) + r3[:, at].astype(f32)
        value, slope = gelu_pair(total[:rows] + bias[:, at])
        grad = (total[rows:] * slope).astype(bf16)
        pair[p, :rows, :] = value.astype(bf16)
        pair[p, rows:, :] = grad
        pre_grad[:, at] = grad


def input_kernel(place, g0, g1, g2, g3, up, keep, s1, s2, s3, same, parts):
    rows = g0.shape[0]
    row = place[0]
    for i in range(4):
        same[i] = place[i]
    group = jnp.concatenate([g0[...], g1[...], g2[...], g3[...]], axis=0)
    tile = 256
    for t in range(up.shape[0] // tile):
        at = slice(t * tile, (t + 1) * tile)
        term = dot(group, up[at, :], ((1,), (1,)))
        for k in range(SIDE):
            parts[k, :, at] = term[k * rows : (k + 1) * rows]
    keep[...] = parts[row]
    for k, send in ((1, s1), (2, s2), (3, s3)):
        send[...] = parts[lax.rem(row + (SIDE - k), SIDE)].astype(bf16)


def weight_kernel(place, *refs):
    pieces, pairs = refs[:8], refs[8:12]
    up_keep, down_keep, bias_keep, send = refs[12:16]
    act_s, grad_s = refs[16:18]
    row, x, z, core = place[0], place[1], place[2], place[3]
    whole = pieces[0].shape[0]
    rows = whole // SIDE
    spot = {0: 0, 1: 1, 3: 2}
    for m in range(SIDE):
        block = lax.rem(row + (SIDE - m), SIDE)
        for dz in range(ZL):
            for dx in range(NX):
                peer = lax.rem(z + dz, ZL) * NX + lax.rem(x + (NX - dx), NX)
                if dx == 2:
                    at = (6 * whole + dz * (whole // 2)) + (
                        lax.div(block, 2) * whole + lax.rem(block, 2) * rows
                    )
                else:
                    at = (dz * 3 + spot[dx]) * whole + block * rows
                at = pl.multiple_of(at, rows)
                act_s[pl.ds(at, rows), :] = pairs[m][peer, :rows, :]
                grad_s[pl.ds(at, rows), :] = pairs[m][peer, rows:, :]
    narrow, width = up_keep.shape
    own = pl.multiple_of(core * narrow, narrow)
    other = pl.multiple_of((1 - core) * narrow, narrow)
    send[2 * narrow :, :] = jnp.zeros((send.shape[0] - 2 * narrow, width), f32)
    for at, out, i in ((own, bias_keep, 0), (other, send, 2 * narrow)):
        total = jnp.sum(grad_s[:, pl.ds(at, narrow)].astype(f32), axis=0, keepdims=True)
        out[i : i + 1, :narrow] = total
    tile = 256
    for scratch, offset, keep, to in (
        (grad_s, 0, up_keep, 0),
        (act_s, width, down_keep, narrow),
    ):
        left = jnp.concatenate(
            [scratch[:, pl.ds(own, narrow)].T, scratch[:, pl.ds(other, narrow)].T], axis=0
        )
        for t in range(width // tile):
            at = slice(t * tile, (t + 1) * tile)
            src = slice(offset + t * tile, offset + (t + 1) * tile)
            acc = None
            for q in range(4):
                right = jnp.concatenate([pieces[2 * q][:, src], pieces[2 * q + 1][:, src]], axis=0)
                term = dot(left[:, q * 2 * whole : (q + 1) * 2 * whole], right, ((1,), (0,)))
                acc = term if acc is None else acc + term
            keep[:, at] = acc[:narrow]
            send[to : to + narrow, at] = acc[narrow:]


def last_kernel(up_keep, down_keep, bias_keep, got, keep, i1, i2, i3, up, down, bias, inp):
    inp[...] = (
        keep[...] + i1[...].astype(f32) + i2[...].astype(f32) + i3[...].astype(f32)
    ).astype(bf16)
    narrow = up_keep.shape[0]
    up[...] = (up_keep[...] + got[:narrow, :]).T
    down[...] = down_keep[...] + got[narrow : 2 * narrow, :]
    bias[...] = bias_keep[...] + got[2 * narrow : 2 * narrow + 1, :narrow]


def local(tokens, up_weight, up_bias, down_weight, out_grad, bucket_lengths):
    rows, width = out_grad.shape
    hidden = up_weight.shape[1]
    narrow = hidden // (PEERS * NC)
    row = lax.axis_index("row")
    dp = lax.axis_index("dp")
    core, x, z = dp % NC, (dp // NC) % NX, dp // (NC * NX)
    place = jnp.stack([row, x, z, core]).astype(jnp.int32)

    (both,) = call(
        mask_kernel,
        (shape((rows, 2 * width), bf16),),
        (),
        (0, MASK << 20),
        bucket_lengths,
        tokens,
        out_grad,
        smem=1,
        name="mask",
    )
    (place,) = call(
        near_kernel,
        (shape((4,), jnp.int32),),
        (),
        (0, 1 << 20),
        place,
        up_weight,
        down_weight,
        smem=1,
        tail=1,
        name="near",
    )
    c2 = shift(both, "col", 2)
    c1, c3 = shift(both, "col", 1), shift(both, "col", 3)
    send = shape((2 * rows, hidden), bf16)
    group, keep, s1, s2, s3 = call(
        first_kernel,
        (shape((SIDE * rows, 2 * width), bf16), shape((2 * rows, hidden), f32), send, send, send),
        [pltpu.VMEM((SIDE, 2 * rows, hidden), f32)],
        (8 * SIDE * rows * width * hidden, 8 << 20),
        place,
        both,
        c1,
        c2,
        c3,
        up_weight,
        down_weight,
        smem=1,
        name="first",
    )
    r2 = shift(s2, "row", 2)
    r1, r3 = shift(s1, "row", 1), shift(s3, "row", 3)

    half = SIDE * rows // 2
    other = flip_z(group)
    after, before = shift_x(group, 1), shift_x(group, -1)

    pair, pre_grad = call(
        gelu_kernel,
        (shape((PEERS, 2 * rows, NC * narrow), bf16), shape((rows, hidden), bf16)),
        (),
        (1 << 22, GELU << 20),
        keep,
        r1,
        r2,
        r3,
        up_bias.reshape(1, hidden),
        name="gelu",
    )
    other, pre_grad = lax.optimization_barrier((other, pre_grad))
    after_o, before_o = shift_x(other, 1), shift_x(other, -1)
    groups = [[NC * p + c for p in range(PEERS)] for c in range(NC)]
    pair = lax.all_to_all(pair, "dp", 0, 0, axis_index_groups=groups)
    g2 = shift(pre_grad, "row", 2)
    g1, g3 = shift(pre_grad, "row", 1), shift(pre_grad, "row", 3)
    after_o, before_o, g1, g2, g3 = lax.optimization_barrier((after_o, before_o, g1, g2, g3))
    far_a = shift_x(jnp.concatenate([after[:half], after_o[:half]], axis=0), 1)
    far_b = shift_x(jnp.concatenate([before[half:], before_o[half:]], axis=0), -1)
    pieces = [group, after, before, other, after_o, before_o, far_a, far_b]
    p2 = shift(pair, "row", 2)
    p1, p3 = shift(pair, "row", 1), shift(pair, "row", 3)

    send = shape((rows, width), bf16)
    keep, s1, s2, s3, place = call(
        input_kernel,
        (shape((rows, width), f32), send, send, send, shape((4,), jnp.int32)),
        [pltpu.VMEM((SIDE, rows, width), f32)],
        (2 * SIDE * rows * width * hidden, INPUT << 20),
        place,
        pre_grad,
        g1,
        g2,
        g3,
        up_weight,
        smem=1,
        tail=1,
        name="input",
    )
    i2 = shift(s2, "col", -2)
    i1, i3 = shift(s1, "col", -1), shift(s3, "col", -3)

    block, line = shape((narrow, width), f32), shape((1, narrow), f32)
    count = PEERS * SIDE * rows
    up_keep, down_keep, bias_keep, send = call(
        weight_kernel,
        (block, block, line, shape((2 * narrow + 8, width), f32)),
        [pltpu.VMEM((count, NC * narrow), bf16)] * 2,
        (8 * count * width * narrow * NC, WEIGHT << 20),
        place,
        *pieces,
        pair,
        p1,
        p2,
        p3,
        smem=1,
        name="weight",
    )
    send, i1, i2, i3 = lax.optimization_barrier((send, i1, i2, i3))
    up_grad, down_grad, bias_grad, input_grad = call(
        last_kernel,
        (shape((width, narrow), f32), block, line, shape((rows, width), bf16)),
        (),
        (1 << 20, 3 << 20),
        up_keep,
        down_keep,
        bias_keep,
        flip_core(send),
        keep,
        i1,
        i2,
        i3,
        name="last",
    )
    return (
        input_grad,
        up_grad.reshape(width, 1, narrow),
        bias_grad,
        down_grad.reshape(1, narrow, width),
    )


def solution(mesh):
    return jax.shard_map(
        local,
        mesh=mesh,
        in_specs=(
            P(("dp", "col"), "row"),
            P("row", "col"),
            P("col"),
            P("col", "row"),
            P(("dp", "col"), "row"),
            P(("dp", "col")),
        ),
        out_specs=(
            P(("dp", "col"), "row"),
            P("row", "col", "dp"),
            P("col", "dp"),
            P("col", "dp", "row"),
        ),
        check_vma=False,
    )
```

time: 132 us -> 95.9 us (0.73)
  the two profiles are of different devices: /device:TPU:6 before, /device:TPU:1 now
where the time goes in v2:
time: 95.9 us; the launch traced here: 95.2 us
  starting transfers between devices  53.6 us (56%)
  waiting for transfers between devices  18.7 us (19%)
  Pallas kernels  11.4 us (12%)
  local copies, waits for them, and re-layouts  8.32 us (9%)
  other arithmetic  1.76 us (2%)
  between operations  1.41 us (1%)
    ppermute x15, starting transfers between devices, shift(): lax.ppermute(array, axis, [(i, (i + by) % count) for i in range(count)])  32.6 us
    ppermute x8, starting transfers between devices, move(): return lax.ppermute(array, 'dp', pairs)  17 us
    ppermute x15, waiting for transfers between devices, shift(): lax.ppermute(array, axis, [(i, (i + by) % count) for i in range(count)])  13.6 us
    pallas_call x7, Pallas kernels, call(): pl.pallas_call(kernel, out_shape=outs, in_specs=[SMEM] * smem + [VMEM] *...  11.4 us
    unnamed x16, local copies, waits for them, and re-layouts  8.25 us
    ppermute x8, waiting for transfers between devices, move(): return lax.ppermute(array, 'dp', pairs)  5.04 us
    all_to_all x1, starting transfers between devices, local(): pair = lax.all_to_all(pair, 'dp', 0, 0, axis_index_groups=groups)  4 us
  transfers between devices with their start and end apart: 24, of which 11 were waited for; matrix products, arithmetic and copies ran while one was open for 2% of the time, Pallas kernels for 8%

profile of v2, /device:TPU:1, one launch (start us, length us, event | category | flops | bytes accessed | tf_op | source)
XLA Modules:
  0.0 95.2 jit_solution(626246912597589293)
XLA Ops:
  3.0 6.9 %collective-permute-start.2 = (bf16[32,2048]{1,0:T(8,128)(2,1)S(1)}, bf16[32,2048]{1,0:T(8,128)(2,1)S(1)}, u32[]{:S(2)}, u32[]{:S(2)}) collective-permute-start(bf16[32,2048]{1,0:T(8,128)(2,1)S(1)} %mask.1.b0), channel_id=1, source_target_pairs={{0,3},{1,0},{2,1},{3,2},{4,7},{5,4},{6,5},{7,6},{8,11},{9,8},{10,9... | collective-permute-start | bytes 393224 | tf_op jit(solution)/shard_map/ppermute | solution.py:53
  10.9 2.3 %collective-permute-start = (bf16[32,2048]{1,0:T(8,128)(2,1)S(1)}, bf16[32,2048]{1,0:T(8,128)(2,1)S(1)}, u32[]{:S(2)}, u32[]{:S(2)}) collective-permute-start(bf16[32,2048]{1,0:T(8,128)(2,1)S(1)} %mask.1.b0), channel_id=1, source_target_pairs={{0,1},{1,2},{2,3},{3,0},{4,5},{5,6},{6,7},{7,4},{8,9},{9,10},{10,1... | collective-permute-start | bytes 393224 | tf_op jit(solution)/shard_map/ppermute | solution.py:53
  13.2 2.2 %copy-done = bf16[1024,2048]{1,0:T(8,128)(2,1)S(1)} copy-done((bf16[1024,2048]{1,0:T(8,128)(2,1)S(1)}, bf16[1024,2048]{1,0:T(8,128)(2,1)}, u32[]{:S(2)}) %copy-start) | copy-done | bytes 4194328
  15.4 2.2 %copy-done.3 = bf16[2048,1024]{1,0:T(8,128)(2,1)S(1)} copy-done((bf16[2048,1024]{1,0:T(8,128)(2,1)S(1)}, bf16[2048,1024]{1,0:T(8,128)(2,1)}, u32[]{:S(2)}) %copy-start.3) | copy-done | bytes 4194328
  18.8 2.2 %collective-permute-done.1.b2 = bf16[32,2048]{1,0:T(8,128)(2,1)S(1)} collective-permute-done((bf16[32,2048]{1,0:T(8,128)(2,1)S(1)}, bf16[32,2048]{1,0:T(8,128)(2,1)S(1)}, u32[]{:S(2)}, u32[]{:S(2)}) %collective-permute-start.1) | collective-permute-done | bytes 131104 | tf_op jit(solution)/shard_map/ppermute | solution.py:53
  21.2 2.8 %first.1 = (bf16[128,2048]{1,0:T(8,128)(2,1)S(1)}, f32[64,2048]{1,0:T(8,128)S(1)}, bf16[64,2048]{1,0:T(8,128)(2,1)S(1)}, bf16[64,2048]{1,0:T(8,128)(2,1)S(1)}, bf16[64,2048]{1,0:T(8,128)(2,1)S(1)}) custom-call(s32[4]{0:T(128)S(1)} %near.1.place, bf16[32,2048]{1,0:T(8,128)(2,1)S(1)} %mask.1.b0, bf16[32,2048]{1,0:T(8,128)(2,1)S(1)} %collective-permute-done.b1, ...), custom_call_target="tpu_custom_call" | custom-call | flops 2147483648 | bytes 8388608 | tf_op jit(solution)/shard_map/first/pallas_call | solution.py:39
  24.0 3.3 %collective-permute-start.3 = (bf16[128,2048]{1,0:T(8,128)(2,1)S(1)}, bf16[128,2048]{1,0:T(8,128)(2,1)}, u32[]{:S(2)}, u32[]{:S(2)}) collective-permute-start(bf16[128,2048]{1,0:T(8,128)(2,1)S(1)} %get-tuple-element.35.refs_0_), channel_id=1, source_target_pairs={{0,128},{16,144},{32,160},{48,176},{64,192},{80,208},{96,224},{112... | collective-permute-start | bytes 1572872 | tf_op jit(solution)/shard_map/ppermute | solution.py:63
  28.6 2.6 %collective-permute-start.5 = (bf16[64,2048]{1,0:T(8,128)(2,1)S(1)}, bf16[64,2048]{1,0:T(8,128)(2,1)S(1)}, u32[]{:S(2)}, u32[]{:S(2)}) collective-permute-start(bf16[64,2048]{1,0:T(8,128)(2,1)S(1)} %get-tuple-element.38), channel_id=1, source_target_pairs={{0,8},{4,12},{8,0},{12,4},{1,9},{5,13},{9,1},{13,5},{2,10},{6,14},... | collective-permute-start | bytes 786440 | tf_op jit(solution)/shard_map/ppermute | solution.py:53
  32.2 2.5 %collective-permute-start.13 = (bf16[128,2048]{1,0:T(8,128)(2,1)S(1)}, bf16[128,2048]{1,0:T(8,128)(2,1)S(1)}, u32[]{:S(2)}, u32[]{:S(2)}) collective-permute-start(bf16[128,2048]{1,0:T(8,128)(2,1)S(1)} %get-tuple-element.35.refs_0_), channel_id=1, source_target_pairs={{0,96},{16,112},{32,0},{48,16},{64,32},{80,48},{96,64},{112,80},{1... | collective-permute-start | bytes 1572872 | tf_op jit(solution)/shard_map/ppermute | solution.py:63
  36.3 5.5 %collective-permute-done.5.r2 = bf16[64,2048]{1,0:T(8,128)(2,1)S(1)} collective-permute-done((bf16[64,2048]{1,0:T(8,128)(2,1)S(1)}, bf16[64,2048]{1,0:T(8,128)(2,1)S(1)}, u32[]{:S(2)}, u32[]{:S(2)}) %collective-permute-start.5) | collective-permute-done | bytes 262176 | tf_op jit(solution)/shard_map/ppermute | solution.py:53
  42.8 2.5 %collective-permute-start.8 = (bf16[128,2048]{1,0:T(8,128)(2,1)}, bf16[128,2048]{1,0:T(8,128)(2,1)S(1)}, u32[]{:S(2)}, u32[]{:S(2)}) collective-permute-start(bf16[128,2048]{1,0:T(8,128)(2,1)} %collective-permute-done.3.refs_3_), channel_id=1, source_target_pairs={{0,96},{16,112},{32,0},{48,16},{64,32},{80,48},{96,64},{112,80},{1... | collective-permute-start | bytes 1572872 | tf_op jit(solution)/shard_map/ppermute | solution.py:63
  45.2 3.2 %collective-permute-start.11 = (bf16[32,2048]{1,0:T(8,128)(2,1)S(1)}, bf16[32,2048]{1,0:T(8,128)(2,1)S(1)}, u32[]{:S(2)}, u32[]{:S(2)}) collective-permute-start(bf16[32,2048]{1,0:T(8,128)(2,1)S(1)} %get-tuple-element.41.g0), channel_id=1, source_target_pairs={{0,12},{4,0},{8,4},{12,8},{1,13},{5,1},{9,5},{13,9},{2,14},{6,2},{... | collective-permute-start | bytes 393224 | tf_op jit(solution)/shard_map/ppermute | solution.py:53
  49.1 4.0 %all-to-all-start = ((bf16[8,64,256]{2,1,0:T(8,128)(2,1)}), bf16[8,64,256]{2,1,0:T(8,128)(2,1)S(1)}, u32[]{:S(2)}, u32[]{:S(2)}) async-start(bf16[8,64,256]{2,1,0:T(8,128)(2,1)} %get-tuple-element.49), calls=%async_computation | async-start | bytes 524288 | tf_op jit(solution)/shard_map/all_to_all | solution.py:271
  53.9 3.2 %collective-permute-done.9.g1 = bf16[32,2048]{1,0:T(8,128)(2,1)S(1)} collective-permute-done((bf16[32,2048]{1,0:T(8,128)(2,1)S(1)}, bf16[32,2048]{1,0:T(8,128)(2,1)S(1)}, u32[]{:S(2)}, u32[]{:S(2)}) %collective-permute-start.9) | collective-permute-done | bytes 131104 | tf_op jit(solution)/shard_map/ppermute | solution.py:53
  57.1 2.7 %collective-permute-done.7.refs_4_ = bf16[128,2048]{1,0:T(8,128)(2,1)S(1)} collective-permute-done((bf16[128,2048]{1,0:T(8,128)(2,1)}, bf16[128,2048]{1,0:T(8,128)(2,1)S(1)}, u32[]{:S(2)}, u32[]{:S(2)}) %collective-permute-start.7) | collective-permute-done | bytes 524320 | tf_op jit(solution)/shard_map/ppermute | solution.py:63
  63.0 3.0 %collective-permute-start.18 = (bf16[8,64,256]{2,1,0:T(8,128)(2,1)S(1)}, bf16[8,64,256]{2,1,0:T(8,128)(2,1)S(1)}, u32[]{:S(2)}, u32[]{:S(2)}) collective-permute-start(bf16[8,64,256]{2,1,0:T(8,128)(2,1)S(1)} %all-to-all-done.refs_8_), channel_id=1, source_target_pairs={{0,12},{4,0},{8,4},{12,8},{1,13},{5,1},{9,5},{13,9},{2,14},{6,2},{... | collective-permute-start | bytes 786440 | tf_op jit(solution)/shard_map/ppermute | solution.py:53
  67.9 2.2 %copy-done.2 = bf16[1024,2048]{1,0:T(8,128)(2,1)S(1)} copy-done((bf16[1024,2048]{1,0:T(8,128)(2,1)S(1)}, bf16[1024,2048]{1,0:T(8,128)(2,1)}, u32[]{:S(2)}) %copy-start.2) | copy-done | bytes 4194328
  70.0 2.5 %input.1 = (f32[32,1024]{1,0:T(8,128)S(1)}, bf16[32,1024]{1,0:T(8,128)(2,1)S(1)}, bf16[32,1024]{1,0:T(8,128)(2,1)S(1)}, bf16[32,1024]{1,0:T(8,128)(2,1)S(1)}, s32[4]{0:T(128)S(1)}) custom-call(s32[4]{0:T(128)S(1)} %near.1.place, bf16[32,2048]{1,0:T(8,128)(2,1)S(1)} %get-tuple-element.41.g0, bf16[32,2048]{1,0:T(8,128)(2,1)S(1)} %collective-permute-done.9.g1, ...), custom_call_target="tpu_custom_call" | custom-call | flops 536870912 | bytes 67108864 | tf_op jit(solution)/shard_map/input/pallas_call | solution.py:39
  73.2 4.5 %collective-permute-start.19 = (bf16[32,1024]{1,0:T(8,128)(2,1)S(1)}, bf16[32,1024]{1,0:T(8,128)(2,1)S(1)}, u32[]{:S(2)}, u32[]{:S(2)}) collective-permute-start(bf16[32,1024]{1,0:T(8,128)(2,1)S(1)} %get-tuple-element.54), channel_id=1, source_target_pairs={{0,3},{1,0},{2,1},{3,2},{4,7},{5,4},{6,5},{7,6},{8,11},{9,8},{10,9... | collective-permute-start | bytes 196616 | tf_op jit(solution)/shard_map/ppermute | solution.py:53
  77.7 1.9 %collective-permute-start.20 = (bf16[32,1024]{1,0:T(8,128)(2,1)S(1)}, bf16[32,1024]{1,0:T(8,128)(2,1)S(1)}, u32[]{:S(2)}, u32[]{:S(2)}) collective-permute-start(bf16[32,1024]{1,0:T(8,128)(2,1)S(1)} %get-tuple-element.55), channel_id=1, source_target_pairs={{0,2},{1,3},{2,0},{3,1},{4,6},{5,7},{6,4},{7,5},{8,10},{9,11},{10,... | collective-permute-start | bytes 196616 | tf_op jit(solution)/shard_map/ppermute | solution.py:53
  79.6 2.3 %collective-permute-start.21 = (bf16[32,1024]{1,0:T(8,128)(2,1)S(1)}, bf16[32,1024]{1,0:T(8,128)(2,1)S(1)}, u32[]{:S(2)}, u32[]{:S(2)}) collective-permute-start(bf16[32,1024]{1,0:T(8,128)(2,1)S(1)} %get-tuple-element.56), channel_id=1, source_target_pairs={{0,1},{1,2},{2,3},{3,0},{4,5},{5,6},{6,7},{7,4},{8,9},{9,10},{10,1... | collective-permute-start | bytes 196616 | tf_op jit(solution)/shard_map/ppermute | solution.py:53
  81.9 2.8 %weight.1 = (f32[128,1024]{1,0:T(8,128)S(1)}, f32[128,1024]{1,0:T(8,128)S(1)}, f32[1,128]{1,0:T(1,128)S(1)}, f32[264,1024]{1,0:T(8,128)S(1)}) custom-call(s32[4]{0:T(128)S(1)} %get-tuple-element.46.place, bf16[128,2048]{1,0:T(8,128)(2,1)S(1)} %get-tuple-element.35.refs_0_, bf16[128,2048]{1,0:T(8,128)(2,1)S(1)} %collective-permute-done.12.refs_1_, ...), custom_call_target="tpu_custom_call" | custom-call | flops 2147483648 | bytes 67108864 | tf_op jit(solution)/shard_map/weight/pallas_call | solution.py:39
  85.5 6.1 %collective-permute-start.22 = (f32[264,1024]{1,0:T(8,128)S(1)}, f32[264,1024]{1,0:T(8,128)S(1)}, u32[]{:S(2)}, u32[]{:S(2)}) collective-permute-start(f32[264,1024]{1,0:T(8,128)S(1)} %get-tuple-element.57), channel_id=1, source_target_pairs={{0,16},{16,0},{32,48},{48,32},{64,80},{80,64},{96,112},{112,96},{1... | collective-permute-start | bytes 3244040 | tf_op jit(solution)/shard_map/ppermute | solution.py:63
  91.7 2.3 %collective-permute-done.22.got = f32[264,1024]{1,0:T(8,128)S(1)} collective-permute-done((f32[264,1024]{1,0:T(8,128)S(1)}, f32[264,1024]{1,0:T(8,128)S(1)}, u32[]{:S(2)}, u32[]{:S(2)}) %collective-permute-start.22) | collective-permute-done | bytes 1081376 | tf_op jit(solution)/shard_map/ppermute | solution.py:63
  (54 shorter events, 18.2 us)
Async XLA Ops:
  3.0 15.8 %collective-permute-start.2 = (bf16[32,2048]{1,0:T(8,128)(2,1)S(1)}, bf16[32,2048]{1,0:T(8,128)(2,1)S(1)}, u32[]{:S(2)}, u32[]{:S(2)}) collective-permute-start(bf16[32,2048]{1,0:T(8,128)(2,1)S(1)} %mask.1.b0), channel_id=1, source_target_pairs={{0,3},{1,0},{2,1},{3,2},{4,7},{5,4},{6,5},{7,6},{8,11},{9,8},{10,9... | collective-permute-start | bytes 393224 | tf_op jit(solution)/shard_map/ppermute | solution.py:53
  9.9 11.1 %collective-permute-start.1 = (bf16[32,2048]{1,0:T(8,128)(2,1)S(1)}, bf16[32,2048]{1,0:T(8,128)(2,1)S(1)}, u32[]{:S(2)}, u32[]{:S(2)}) collective-permute-start(bf16[32,2048]{1,0:T(8,128)(2,1)S(1)} %mask.1.b0), channel_id=1, source_target_pairs={{0,2},{1,3},{2,0},{3,1},{4,6},{5,7},{6,4},{7,5},{8,10},{9,11},{10,... | collective-permute-start | bytes 393224 | tf_op jit(solution)/shard_map/ppermute | solution.py:53
  10.9 10.3 %collective-permute-start = (bf16[32,2048]{1,0:T(8,128)(2,1)S(1)}, bf16[32,2048]{1,0:T(8,128)(2,1)S(1)}, u32[]{:S(2)}, u32[]{:S(2)}) collective-permute-start(bf16[32,2048]{1,0:T(8,128)(2,1)S(1)} %mask.1.b0), channel_id=1, source_target_pairs={{0,1},{1,2},{2,3},{3,0},{4,5},{5,6},{6,7},{7,4},{8,9},{9,10},{10,1... | collective-permute-start | bytes 393224 | tf_op jit(solution)/shard_map/ppermute | solution.py:53
  24.0 18.8 %collective-permute-start.3 = (bf16[128,2048]{1,0:T(8,128)(2,1)S(1)}, bf16[128,2048]{1,0:T(8,128)(2,1)}, u32[]{:S(2)}, u32[]{:S(2)}) collective-permute-start(bf16[128,2048]{1,0:T(8,128)(2,1)S(1)} %get-tuple-element.35.refs_0_), channel_id=1, source_target_pairs={{0,128},{16,144},{32,160},{48,176},{64,192},{80,208},{96,224},{112... | collective-permute-start | bytes 1572872 | tf_op jit(solution)/shard_map/ppermute | solution.py:63
  27.3 7.8 %collective-permute-start.4 = (bf16[64,2048]{1,0:T(8,128)(2,1)S(1)}, bf16[64,2048]{1,0:T(8,128)(2,1)S(1)}, u32[]{:S(2)}, u32[]{:S(2)}) collective-permute-start(bf16[64,2048]{1,0:T(8,128)(2,1)S(1)} %get-tuple-element.37), channel_id=1, source_target_pairs={{0,4},{4,8},{8,12},{12,0},{1,5},{5,9},{9,13},{13,1},{2,6},{6,10},{... | collective-permute-start | bytes 786440 | tf_op jit(solution)/shard_map/ppermute | solution.py:53
  28.6 13.2 %collective-permute-start.5 = (bf16[64,2048]{1,0:T(8,128)(2,1)S(1)}, bf16[64,2048]{1,0:T(8,128)(2,1)S(1)}, u32[]{:S(2)}, u32[]{:S(2)}) collective-permute-start(bf16[64,2048]{1,0:T(8,128)(2,1)S(1)} %get-tuple-element.38), channel_id=1, source_target_pairs={{0,8},{4,12},{8,0},{12,4},{1,9},{5,13},{9,1},{13,5},{2,10},{6,14},... | collective-permute-start | bytes 786440 | tf_op jit(solution)/shard_map/ppermute | solution.py:53
  31.2 10.6 %collective-permute-start.6 = (bf16[64,2048]{1,0:T(8,128)(2,1)S(1)}, bf16[64,2048]{1,0:T(8,128)(2,1)S(1)}, u32[]{:S(2)}, u32[]{:S(2)}) collective-permute-start(bf16[64,2048]{1,0:T(8,128)(2,1)S(1)} %get-tuple-element.39), channel_id=1, source_target_pairs={{0,12},{4,0},{8,4},{12,8},{1,13},{5,1},{9,5},{13,9},{2,14},{6,2},{... | collective-permute-start | bytes 786440 | tf_op jit(solution)/shard_map/ppermute | solution.py:53
  32.2 16.2 %collective-permute-start.13 = (bf16[128,2048]{1,0:T(8,128)(2,1)S(1)}, bf16[128,2048]{1,0:T(8,128)(2,1)S(1)}, u32[]{:S(2)}, u32[]{:S(2)}) collective-permute-start(bf16[128,2048]{1,0:T(8,128)(2,1)S(1)} %get-tuple-element.35.refs_0_), channel_id=1, source_target_pairs={{0,96},{16,112},{32,0},{48,16},{64,32},{80,48},{96,64},{112,80},{1... | collective-permute-start | bytes 1572872 | tf_op jit(solution)/shard_map/ppermute | solution.py:63
  35.0 13.8 %collective-permute-start.12 = (bf16[128,2048]{1,0:T(8,128)(2,1)S(1)}, bf16[128,2048]{1,0:T(8,128)(2,1)S(1)}, u32[]{:S(2)}, u32[]{:S(2)}) collective-permute-start(bf16[128,2048]{1,0:T(8,128)(2,1)S(1)} %get-tuple-element.35.refs_0_), channel_id=1, source_target_pairs={{0,32},{16,48},{32,64},{48,80},{64,96},{80,112},{96,0},{112,16},{1... | collective-permute-start | bytes 1572872 | tf_op jit(solution)/shard_map/ppermute | solution.py:63
  42.8 14.3 %collective-permute-start.8 = (bf16[128,2048]{1,0:T(8,128)(2,1)}, bf16[128,2048]{1,0:T(8,128)(2,1)S(1)}, u32[]{:S(2)}, u32[]{:S(2)}) collective-permute-start(bf16[128,2048]{1,0:T(8,128)(2,1)} %collective-permute-done.3.refs_3_), channel_id=1, source_target_pairs={{0,96},{16,112},{32,0},{48,16},{64,32},{80,48},{96,64},{112,80},{1... | collective-permute-start | bytes 1572872 | tf_op jit(solution)/shard_map/ppermute | solution.py:63
  45.2 14.6 %collective-permute-start.7 = (bf16[128,2048]{1,0:T(8,128)(2,1)}, bf16[128,2048]{1,0:T(8,128)(2,1)S(1)}, u32[]{:S(2)}, u32[]{:S(2)}) collective-permute-start(bf16[128,2048]{1,0:T(8,128)(2,1)} %collective-permute-done.3.refs_3_), channel_id=1, source_target_pairs={{0,32},{16,48},{32,64},{48,80},{64,96},{80,112},{96,0},{112,16},{1... | collective-permute-start | bytes 1572872 | tf_op jit(solution)/shard_map/ppermute | solution.py:63
  45.2 7.9 %collective-permute-start.11 = (bf16[32,2048]{1,0:T(8,128)(2,1)S(1)}, bf16[32,2048]{1,0:T(8,128)(2,1)S(1)}, u32[]{:S(2)}, u32[]{:S(2)}) collective-permute-start(bf16[32,2048]{1,0:T(8,128)(2,1)S(1)} %get-tuple-element.41.g0), channel_id=1, source_target_pairs={{0,12},{4,0},{8,4},{12,8},{1,13},{5,1},{9,5},{13,9},{2,14},{6,2},{... | collective-permute-start | bytes 393224 | tf_op jit(solution)/shard_map/ppermute | solution.py:53
  48.4 5.4 %collective-permute-start.10 = (bf16[32,2048]{1,0:T(8,128)(2,1)S(1)}, bf16[32,2048]{1,0:T(8,128)(2,1)S(1)}, u32[]{:S(2)}, u32[]{:S(2)}) collective-permute-start(bf16[32,2048]{1,0:T(8,128)(2,1)S(1)} %get-tuple-element.41.g0), channel_id=1, source_target_pairs={{0,8},{4,12},{8,0},{12,4},{1,9},{5,13},{9,1},{13,5},{2,10},{6,14},... | collective-permute-start | bytes 393224 | tf_op jit(solution)/shard_map/ppermute | solution.py:53
  48.9 8.3 %collective-permute-start.9 = (bf16[32,2048]{1,0:T(8,128)(2,1)S(1)}, bf16[32,2048]{1,0:T(8,128)(2,1)S(1)}, u32[]{:S(2)}, u32[]{:S(2)}) collective-permute-start(bf16[32,2048]{1,0:T(8,128)(2,1)S(1)} %get-tuple-element.41.g0), channel_id=1, source_target_pairs={{0,4},{4,8},{8,12},{12,0},{1,5},{5,9},{9,13},{13,1},{2,6},{6,10},{... | collective-permute-start | bytes 393224 | tf_op jit(solution)/shard_map/ppermute | solution.py:53
  49.1 13.9 %all-to-all-start = ((bf16[8,64,256]{2,1,0:T(8,128)(2,1)}), bf16[8,64,256]{2,1,0:T(8,128)(2,1)S(1)}, u32[]{:S(2)}, u32[]{:S(2)}) async-start(bf16[8,64,256]{2,1,0:T(8,128)(2,1)} %get-tuple-element.49), calls=%async_computation | async-start | bytes 524288 | tf_op jit(solution)/shard_map/all_to_all | solution.py:271
  60.7 21.2 %collective-permute-start.15 = (bf16[128,2048]{1,0:T(8,128)(2,1)}, bf16[128,2048]{1,0:T(8,128)(2,1)}, u32[]{:S(2)}, u32[]{:S(2)}) collective-permute-start(bf16[128,2048]{1,0:T(8,128)(2,1)} %pad_maximum_fusion.1), channel_id=1, source_target_pairs={{0,96},{16,112},{32,0},{48,16},{64,32},{80,48},{96,64},{112,80},{1... | collective-permute-start | bytes 1572872 | tf_op jit(solution)/shard_map/ppermute | solution.py:63
  62.5 19.4 %collective-permute-start.14 = (bf16[128,2048]{1,0:T(8,128)(2,1)}, bf16[128,2048]{1,0:T(8,128)(2,1)}, u32[]{:S(2)}, u32[]{:S(2)}) collective-permute-start(bf16[128,2048]{1,0:T(8,128)(2,1)} %pad_maximum_fusion), channel_id=1, source_target_pairs={{0,32},{16,48},{32,64},{48,80},{64,96},{80,112},{96,0},{112,16},{1... | collective-permute-start | bytes 1572872 | tf_op jit(solution)/shard_map/ppermute | solution.py:63
  63.0 10.2 %collective-permute-start.18 = (bf16[8,64,256]{2,1,0:T(8,128)(2,1)S(1)}, bf16[8,64,256]{2,1,0:T(8,128)(2,1)S(1)}, u32[]{:S(2)}, u32[]{:S(2)}) collective-permute-start(bf16[8,64,256]{2,1,0:T(8,128)(2,1)S(1)} %all-to-all-done.refs_8_), channel_id=1, source_target_pairs={{0,12},{4,0},{8,4},{12,8},{1,13},{5,1},{9,5},{13,9},{2,14},{6,2},{... | collective-permute-start | bytes 786440 | tf_op jit(solution)/shard_map/ppermute | solution.py:53
  66.0 11.7 %collective-permute-start.17 = (bf16[8,64,256]{2,1,0:T(8,128)(2,1)S(1)}, bf16[8,64,256]{2,1,0:T(8,128)(2,1)S(1)}, u32[]{:S(2)}, u32[]{:S(2)}) collective-permute-start(bf16[8,64,256]{2,1,0:T(8,128)(2,1)S(1)} %all-to-all-done.refs_8_), channel_id=1, source_target_pairs={{0,8},{4,12},{8,0},{12,4},{1,9},{5,13},{9,1},{13,5},{2,10},{6,14},... | collective-permute-start | bytes 786440 | tf_op jit(solution)/shard_map/ppermute | solution.py:53
  67.0 12.6 %collective-permute-start.16 = (bf16[8,64,256]{2,1,0:T(8,128)(2,1)S(1)}, bf16[8,64,256]{2,1,0:T(8,128)(2,1)S(1)}, u32[]{:S(2)}, u32[]{:S(2)}) collective-permute-start(bf16[8,64,256]{2,1,0:T(8,128)(2,1)S(1)} %all-to-all-done.refs_8_), channel_id=1, source_target_pairs={{0,4},{4,8},{8,12},{12,0},{1,5},{5,9},{9,13},{13,1},{2,6},{6,10},{... | collective-permute-start | bytes 786440 | tf_op jit(solution)/shard_map/ppermute | solution.py:53
  73.2 11.5 %collective-permute-start.19 = (bf16[32,1024]{1,0:T(8,128)(2,1)S(1)}, bf16[32,1024]{1,0:T(8,128)(2,1)S(1)}, u32[]{:S(2)}, u32[]{:S(2)}) collective-permute-start(bf16[32,1024]{1,0:T(8,128)(2,1)S(1)} %get-tuple-element.54), channel_id=1, source_target_pairs={{0,3},{1,0},{2,1},{3,2},{4,7},{5,4},{6,5},{7,6},{8,11},{9,8},{10,9... | collective-permute-start | bytes 196616 | tf_op jit(solution)/shard_map/ppermute | solution.py:53
  77.7 7.2 %collective-permute-start.20 = (bf16[32,1024]{1,0:T(8,128)(2,1)S(1)}, bf16[32,1024]{1,0:T(8,128)(2,1)S(1)}, u32[]{:S(2)}, u32[]{:S(2)}) collective-permute-start(bf16[32,1024]{1,0:T(8,128)(2,1)S(1)} %get-tuple-element.55), channel_id=1, source_target_pairs={{0,2},{1,3},{2,0},{3,1},{4,6},{5,7},{6,4},{7,5},{8,10},{9,11},{10,... | collective-permute-start | bytes 196616 | tf_op jit(solution)/shard_map/ppermute | solution.py:53
  79.6 6.0 %collective-permute-start.21 = (bf16[32,1024]{1,0:T(8,128)(2,1)S(1)}, bf16[32,1024]{1,0:T(8,128)(2,1)S(1)}, u32[]{:S(2)}, u32[]{:S(2)}) collective-permute-start(bf16[32,1024]{1,0:T(8,128)(2,1)S(1)} %get-tuple-element.56), channel_id=1, source_target_pairs={{0,1},{1,2},{2,3},{3,0},{4,5},{5,6},{6,7},{7,4},{8,9},{9,10},{10,1... | collective-permute-start | bytes 196616 | tf_op jit(solution)/shard_map/ppermute | solution.py:53
  85.5 8.4 %collective-permute-start.22 = (f32[264,1024]{1,0:T(8,128)S(1)}, f32[264,1024]{1,0:T(8,128)S(1)}, u32[]{:S(2)}, u32[]{:S(2)}) collective-permute-start(f32[264,1024]{1,0:T(8,128)S(1)} %get-tuple-element.57), channel_id=1, source_target_pairs={{0,16},{16,0},{32,48},{48,32},{64,80},{80,64},{96,112},{112,96},{1... | collective-permute-start | bytes 3244040 | tf_op jit(solution)/shard_map/ppermute | solution.py:63
  (8 other events, 38.4 us)

commit v3 on v2

--- a/solution.py
+++ b/solution.py
@@ -75,19 +75,12 @@
     return move(array, lambda z, x, c: (z, x, 1 - c))
 
 
-def mask_kernel(lengths, tokens, out_grad, both):
-    rows, width = tokens.shape
-    live = lax.broadcasted_iota(jnp.int32, (rows, width), 0) < lengths[0]
-    both[:, :width] = tokens[...]
-    both[:, width:] = jnp.where(live, out_grad[...], jnp.zeros_like(out_grad))
-
-
 def near_kernel(place, up, down, same):
     for i in range(4):
         same[i] = place[i]
 
 
-def first_kernel(place, b0, b1, b2, b3, up, down, group, keep, s1, s2, s3, parts):
+def first_kernel(place, b0, b1, b2, b3, up, down, group, keep, send, parts):
     rows, both = b0.shape
     width, hidden = up.shape
     row = place[0]
@@ -103,16 +96,18 @@
             parts[k, :rows, at] = pre[own]
             parts[k, rows:, at] = act[own]
     keep[...] = parts[row]
-    for k, send in ((1, s1), (2, s2), (3, s3)):
-        send[...] = parts[lax.rem(row + k, SIDE)].astype(bf16)
-
-
-def gelu_kernel(keep, r1, r2, r3, bias, pair, pre_grad):
+    send[...] = parts[...].astype(bf16)
+
+
+def gelu_kernel(place, keep, got, bias, pair, pre_grad):
+    others = [lax.rem(place[0] + k, SIDE) for k in (1, 2, 3)]
     rows = keep.shape[0] // 2
     wide = pair.shape[2]
     for p in range(PEERS):
         at = slice(p * wide, (p + 1) * wide)
-        total = keep[:, at] + r1[:, at].astype(f32) + r2[:, at].astype(f32) + r3[:, at].astype(f32)
+        total = keep[:, at]
+        for other in others:
+            total = total + got[other, :, at].astype(f32)
         value, slope = gelu_pair(total[:rows] + bias[:, at])
         grad = (total[rows:] * slope).astype(bf16)
         pair[p, :rows, :] = value.astype(bf16)
@@ -205,17 +200,9 @@
     core, x, z = dp % NC, (dp // NC) % NX, dp // (NC * NX)
     place = jnp.stack([row, x, z, core]).astype(jnp.int32)
 
-    (both,) = call(
-        mask_kernel,
-        (shape((rows, 2 * width), bf16),),
-        (),
-        (0, MASK << 20),
-        bucket_lengths,
-        tokens,
-        out_grad,
-        smem=1,
-        name="mask",
-    )
+    live = lax.broadcasted_iota(jnp.int32, (rows, 2 * width), 0) < bucket_lengths[0]
+    live = live | (lax.broadcasted_iota(jnp.int32, (rows, 2 * width), 1) < width)
+    both = jnp.where(live, jnp.concatenate([tokens, out_grad], axis=1), jnp.zeros((), bf16))
     (place,) = call(
         near_kernel,
         (shape((4,), jnp.int32),),
@@ -230,10 +217,10 @@
     )
     c2 = shift(both, "col", 2)
     c1, c3 = shift(both, "col", 1), shift(both, "col", 3)
-    send = shape((2 * rows, hidden), bf16)
-    group, keep, s1, s2, s3 = call(
+    send = shape((SIDE, 2 * rows, hidden), bf16)
+    group, keep, send = call(
         first_kernel,
-        (shape((SIDE * rows, 2 * width), bf16), shape((2 * rows, hidden), f32), send, send, send),
+        (shape((SIDE * rows, 2 * width), bf16), shape((2 * rows, hidden), f32), send),
         [pltpu.VMEM((SIDE, 2 * rows, hidden), f32)],
         (8 * SIDE * rows * width * hidden, 8 << 20),
         place,
@@ -246,8 +233,7 @@
         smem=1,
         name="first",
     )
-    r2 = shift(s2, "row", 2)
-    r1, r3 = shift(s1, "row", 1), shift(s3, "row", 3)
+    got = lax.all_to_all(send, "row", 0, 0)
 
     half = SIDE * rows // 2
     other = flip_z(group)
@@ -258,11 +244,11 @@
         (shape((PEERS, 2 * rows, NC * narrow), bf16), shape((rows, hidden), bf16)),
         (),
         (1 << 22, GELU << 20),
+        place,
         keep,
-        r1,
-        r2,
-        r3,
+        got,
         up_bias.reshape(1, hidden),
+        smem=1,
         name="gelu",
     )
     other, pre_grad = lax.optimization_barrier((other, pre_grad))
@@ -271,7 +257,9 @@
     pair = lax.all_to_all(pair, "dp", 0, 0, axis_index_groups=groups)
     g2 = shift(pre_grad, "row", 2)
     g1, g3 = shift(pre_grad, "row", 1), shift(pre_grad, "row", 3)
-    after_o, before_o, g1, g2, g3 = lax.optimization_barrier((after_o, before_o, g1, g2, g3))
+    after_o, before_o, g1, g2, g3, pair = lax.optimization_barrier(
+        (after_o, before_o, g1, g2, g3, pair)
+    )
     far_a = shift_x(jnp.concatenate([after[:half], after_o[:half]], axis=0), 1)
     far_b = shift_x(jnp.concatenate([before[half:], before_o[half:]], axis=0), -1)
     pieces = [group, after, before, other, after_o, before_o, far_a, far_b]

time: 95.9 us -> 93.6 us (0.976)
  local copies, waits for them, and re-layouts: 8.32 us -> 6.65 us
  waiting for transfers between devices: 18.7 us -> 17.4 us
  Pallas kernels: 11.4 us -> 12.6 us
    ppermute x15 -> x12, starting transfers between devices: 32.6 us -> 24.9 us  [shift(): lax.ppermute(array, axis, [(i, (i + by) % count) for i in range(count)])]
    all_to_all x0 -> x1, waiting for transfers between devices: none -> 6.24 us  [local(): got = lax.all_to_all(send, 'row', 0, 0)]
    ppermute x15 -> x12, waiting for transfers between devices: 13.6 us -> 8.19 us  [shift(): lax.ppermute(array, axis, [(i, (i + by) % count) for i in range(count)])]
    all_to_all x0 -> x1, starting transfers between devices: none -> 4.26 us  [local(): got = lax.all_to_all(send, 'row', 0, 0)]
    all_to_all x1, starting transfers between devices: 4 us -> 8.08 us  [local(): pair = lax.all_to_all(pair, 'dp', 0, 0, axis_index_groups=groups)]
    ppermute x8, waiting for transfers between devices: 5.04 us -> 3.01 us  [move(): return lax.ppermute(array, 'dp', pairs)]
    unnamed x16 -> x12, local copies, waits for them, and re-layouts: 8.25 us -> 6.58 us
    pallas_call x7 -> x6, Pallas kernels: 11.4 us -> 12.6 us  [call(): pl.pallas_call(kernel, out_shape=outs, in_specs=[SMEM] * smem + [VMEM] *...]
  transfers between devices with their start and end apart: 24 -> 22, of which waited for: 11 -> 8; matrix products, arithmetic and copies ran while one was open for 2% -> 0% of each run, Pallas kernels for 8% -> 8%
where the time goes in v3:
time: 93.6 us; the launch traced here: 93.2 us
  starting transfers between devices  53.9 us (58%)
  waiting for transfers between devices  17.4 us (19%)
  Pallas kernels  12.6 us (13%)
  local copies, waits for them, and re-layouts  6.65 us (7%)
  between operations  1.45 us (2%)
  other arithmetic  1.15 us (1%)
    ppermute x12, starting transfers between devices, shift(): lax.ppermute(array, axis, [(i, (i + by) % count) for i in range(count)])  24.9 us
    ppermute x8, starting transfers between devices, move(): return lax.ppermute(array, 'dp', pairs)  16.6 us
    pallas_call x6, Pallas kernels, call(): pl.pallas_call(kernel, out_shape=outs, in_specs=[SMEM] * smem + [VMEM] *...  12.6 us
    ppermute x12, waiting for transfers between devices, shift(): lax.ppermute(array, axis, [(i, (i + by) % count) for i in range(count)])  8.19 us
    all_to_all x1, starting transfers between devices, local(): pair = lax.all_to_all(pair, 'dp', 0, 0, axis_index_groups=groups)  8.08 us
    unnamed x12, local copies, waits for them, and re-layouts  6.58 us
    all_to_all x1, waiting for transfers between devices, local(): got = lax.all_to_all(send, 'row', 0, 0)  6.24 us
    all_to_all x1, starting transfers between devices, local(): got = lax.all_to_all(send, 'row', 0, 0)  4.26 us
  transfers between devices with their start and end apart: 22, of which 8 were waited for; matrix products, arithmetic and copies ran while one was open for 0% of the time, Pallas kernels for 8%

profile of v3, /device:TPU:1, one launch (start us, length us, event | category | flops | bytes accessed | tf_op | source)
XLA Modules:
  0.0 93.2 jit_solution(2265300901862525203)
XLA Ops:
  2.3 6.9 %collective-permute-start.2 = (bf16[32,2048]{1,0:T(8,128)(2,1)S(1)}, bf16[32,2048]{1,0:T(8,128)(2,1)S(1)}, u32[]{:S(2)}, u32[]{:S(2)}) collective-permute-start(bf16[32,2048]{1,0:T(8,128)(2,1)S(1)} %or_select_fusion.b0), channel_id=1, source_target_pairs={{0,3},{1,0},{2,1},{3,2},{4,7},{5,4},{6,5},{7,6},{8,11},{9,8},{10,9... | collective-permute-start | bytes 393224 | tf_op jit(solution)/shard_map/ppermute | solution.py:53
  10.2 2.3 %collective-permute-start = (bf16[32,2048]{1,0:T(8,128)(2,1)S(1)}, bf16[32,2048]{1,0:T(8,128)(2,1)S(1)}, u32[]{:S(2)}, u32[]{:S(2)}) collective-permute-start(bf16[32,2048]{1,0:T(8,128)(2,1)S(1)} %or_select_fusion.b0), channel_id=1, source_target_pairs={{0,1},{1,2},{2,3},{3,0},{4,5},{5,6},{6,7},{7,4},{8,9},{9,10},{10,1... | collective-permute-start | bytes 393224 | tf_op jit(solution)/shard_map/ppermute | solution.py:53
  12.5 2.2 %copy-done = bf16[1024,2048]{1,0:T(8,128)(2,1)S(1)} copy-done((bf16[1024,2048]{1,0:T(8,128)(2,1)S(1)}, bf16[1024,2048]{1,0:T(8,128)(2,1)}, u32[]{:S(2)}) %copy-start) | copy-done | bytes 4194328
  14.7 2.2 %copy-done.3 = bf16[2048,1024]{1,0:T(8,128)(2,1)S(1)} copy-done((bf16[2048,1024]{1,0:T(8,128)(2,1)S(1)}, bf16[2048,1024]{1,0:T(8,128)(2,1)}, u32[]{:S(2)}) %copy-start.3) | copy-done | bytes 4194328
  18.1 2.2 %collective-permute-done.1.b2 = bf16[32,2048]{1,0:T(8,128)(2,1)S(1)} collective-permute-done((bf16[32,2048]{1,0:T(8,128)(2,1)S(1)}, bf16[32,2048]{1,0:T(8,128)(2,1)S(1)}, u32[]{:S(2)}, u32[]{:S(2)}) %collective-permute-start.1) | collective-permute-done | bytes 131104 | tf_op jit(solution)/shard_map/ppermute | solution.py:53
  20.5 3.7 %first.1 = (bf16[128,2048]{1,0:T(8,128)(2,1)}, f32[64,2048]{1,0:T(8,128)S(1)}, bf16[4,64,2048]{2,1,0:T(8,128)(2,1)}) custom-call(s32[4]{0:T(128)S(1)} %near.1.place, bf16[32,2048]{1,0:T(8,128)(2,1)S(1)} %or_select_fusion.b0, bf16[32,2048]{1,0:T(8,128)(2,1)S(1)} %collective-permute-done.b1, bf16[32,2048]{1,0:T(8,128)(2,1)S(1)} %collective-permute-done.1.b2, ...), custom_call_target="tpu_custom_call" | custom-call | flops 2147483648 | bytes 8388608 | tf_op jit(solution)/shard_map/first/pallas_call | solution.py:39
  24.2 4.3 %all-to-all-start = ((bf16[4,64,2048]{2,1,0:T(8,128)(2,1)}), bf16[4,64,2048]{2,1,0:T(8,128)(2,1)S(1)}, u32[]{:S(2)}, u32[]{:S(2)}) async-start(bf16[4,64,2048]{2,1,0:T(8,128)(2,1)} %get-tuple-element.36), calls=%async_computation | async-start | bytes 2097152 | tf_op jit(solution)/shard_map/all_to_all | solution.py:236
  28.4 3.1 %collective-permute-start.3 = (bf16[128,2048]{1,0:T(8,128)(2,1)}, bf16[128,2048]{1,0:T(8,128)(2,1)}, u32[]{:S(2)}, u32[]{:S(2)}) collective-permute-start(bf16[128,2048]{1,0:T(8,128)(2,1)} %get-tuple-element.34.refs_0_), channel_id=1, source_target_pairs={{0,128},{16,144},{32,160},{48,176},{64,192},{80,208},{96,224},{112... | collective-permute-start | bytes 1572872 | tf_op jit(solution)/shard_map/ppermute | solution.py:63
  31.6 2.5 %collective-permute-start.10 = (bf16[128,2048]{1,0:T(8,128)(2,1)}, bf16[128,2048]{1,0:T(8,128)(2,1)S(1)}, u32[]{:S(2)}, u32[]{:S(2)}) collective-permute-start(bf16[128,2048]{1,0:T(8,128)(2,1)} %get-tuple-element.34.refs_0_), channel_id=1, source_target_pairs={{0,96},{16,112},{32,0},{48,16},{64,32},{80,48},{96,64},{112,80},{1... | collective-permute-start | bytes 1572872 | tf_op jit(solution)/shard_map/ppermute | solution.py:63
  34.0 6.2 %all-to-all-done.got = bf16[4,64,2048]{2,1,0:T(8,128)(2,1)S(1)} async-done(((bf16[4,64,2048]{2,1,0:T(8,128)(2,1)}), bf16[4,64,2048]{2,1,0:T(8,128)(2,1)S(1)}, u32[]{:S(2)}, u32[]{:S(2)}) %all-to-all-start) | async-done | bytes 1048608 | tf_op jit(solution)/shard_map/all_to_all | solution.py:236
  42.5 2.4 %collective-permute-start.5 = (bf16[128,2048]{1,0:T(8,128)(2,1)}, bf16[128,2048]{1,0:T(8,128)(2,1)S(1)}, u32[]{:S(2)}, u32[]{:S(2)}) collective-permute-start(bf16[128,2048]{1,0:T(8,128)(2,1)} %collective-permute-done.3.refs_3_), channel_id=1, source_target_pairs={{0,96},{16,112},{32,0},{48,16},{64,32},{80,48},{96,64},{112,80},{1... | collective-permute-start | bytes 1572872 | tf_op jit(solution)/shard_map/ppermute | solution.py:63
  44.9 8.1 %all-to-all-start.1 = ((bf16[8,64,256]{2,1,0:T(8,128)(2,1)}), bf16[8,64,256]{2,1,0:T(8,128)(2,1)S(1)}, u32[]{:S(2)}, u32[]{:S(2)}) async-start(bf16[8,64,256]{2,1,0:T(8,128)(2,1)} %get-tuple-element.40), calls=%async_computation.1 | async-start | bytes 524288 | tf_op jit(solution)/shard_map/all_to_all | solution.py:257
  55.1 2.0 %collective-permute-done.8.g3 = bf16[32,2048]{1,0:T(8,128)(2,1)S(1)} collective-permute-done((bf16[32,2048]{1,0:T(8,128)(2,1)S(1)}, bf16[32,2048]{1,0:T(8,128)(2,1)S(1)}, u32[]{:S(2)}, u32[]{:S(2)}) %collective-permute-start.8) | collective-permute-done | bytes 131104 | tf_op jit(solution)/shard_map/ppermute | solution.py:53
  57.1 2.2 %collective-permute-done.7.g2 = bf16[32,2048]{1,0:T(8,128)(2,1)S(1)} collective-permute-done((bf16[32,2048]{1,0:T(8,128)(2,1)S(1)}, bf16[32,2048]{1,0:T(8,128)(2,1)S(1)}, u32[]{:S(2)}, u32[]{:S(2)}) %collective-permute-start.7) | collective-permute-done | bytes 131104 | tf_op jit(solution)/shard_map/ppermute | solution.py:53
  59.3 1.6 %collective-permute-done.6.g1 = bf16[32,2048]{1,0:T(8,128)(2,1)S(1)} collective-permute-done((bf16[32,2048]{1,0:T(8,128)(2,1)S(1)}, bf16[32,2048]{1,0:T(8,128)(2,1)S(1)}, u32[]{:S(2)}, u32[]{:S(2)}) %collective-permute-start.6) | collective-permute-done | bytes 131104 | tf_op jit(solution)/shard_map/ppermute | solution.py:53
  61.0 2.7 %collective-permute-start.12 = (bf16[128,2048]{1,0:T(8,128)(2,1)S(1)}, bf16[128,2048]{1,0:T(8,128)(2,1)S(1)}, u32[]{:S(2)}, u32[]{:S(2)}) collective-permute-start(bf16[128,2048]{1,0:T(8,128)(2,1)S(1)} %pad_maximum_fusion.1), channel_id=1, source_target_pairs={{0,96},{16,112},{32,0},{48,16},{64,32},{80,48},{96,64},{112,80},{1... | collective-permute-start | bytes 1572872 | tf_op jit(solution)/shard_map/ppermute | solution.py:63
  66.2 2.2 %copy-done.2 = bf16[1024,2048]{1,0:T(8,128)(2,1)S(1)} copy-done((bf16[1024,2048]{1,0:T(8,128)(2,1)S(1)}, bf16[1024,2048]{1,0:T(8,128)(2,1)}, u32[]{:S(2)}) %copy-start.2) | copy-done | bytes 4194328
  68.4 2.4 %input.1 = (f32[32,1024]{1,0:T(8,128)S(1)}, bf16[32,1024]{1,0:T(8,128)(2,1)S(1)}, bf16[32,1024]{1,0:T(8,128)(2,1)S(1)}, bf16[32,1024]{1,0:T(8,128)(2,1)S(1)}, s32[4]{0:T(128)S(1)}) custom-call(s32[4]{0:T(128)S(1)} %near.1.place, bf16[32,2048]{1,0:T(8,128)(2,1)S(1)} %get-tuple-element.38.g0, bf16[32,2048]{1,0:T(8,128)(2,1)S(1)} %collective-permute-done.6.g1, ...), custom_call_target="tpu_custom_call" | custom-call | flops 536870912 | bytes 67108864 | tf_op jit(solution)/shard_map/input/pallas_call | solution.py:39
  70.9 4.0 %collective-permute-start.16 = (bf16[32,1024]{1,0:T(8,128)(2,1)S(1)}, bf16[32,1024]{1,0:T(8,128)(2,1)S(1)}, u32[]{:S(2)}, u32[]{:S(2)}) collective-permute-start(bf16[32,1024]{1,0:T(8,128)(2,1)S(1)} %get-tuple-element.52), channel_id=1, source_target_pairs={{0,3},{1,0},{2,1},{3,2},{4,7},{5,4},{6,5},{7,6},{8,11},{9,8},{10,9... | collective-permute-start | bytes 196616 | tf_op jit(solution)/shard_map/ppermute | solution.py:53
  74.9 2.5 %collective-permute-start.17 = (bf16[32,1024]{1,0:T(8,128)(2,1)S(1)}, bf16[32,1024]{1,0:T(8,128)(2,1)S(1)}, u32[]{:S(2)}, u32[]{:S(2)}) collective-permute-start(bf16[32,1024]{1,0:T(8,128)(2,1)S(1)} %get-tuple-element.53), channel_id=1, source_target_pairs={{0,2},{1,3},{2,0},{3,1},{4,6},{5,7},{6,4},{7,5},{8,10},{9,11},{10,... | collective-permute-start | bytes 196616 | tf_op jit(solution)/shard_map/ppermute | solution.py:53
  77.4 3.7 %collective-permute-start.18 = (bf16[32,1024]{1,0:T(8,128)(2,1)S(1)}, bf16[32,1024]{1,0:T(8,128)(2,1)S(1)}, u32[]{:S(2)}, u32[]{:S(2)}) collective-permute-start(bf16[32,1024]{1,0:T(8,128)(2,1)S(1)} %get-tuple-element.54), channel_id=1, source_target_pairs={{0,1},{1,2},{2,3},{3,0},{4,5},{5,6},{6,7},{7,4},{8,9},{9,10},{10,1... | collective-permute-start | bytes 196616 | tf_op jit(solution)/shard_map/ppermute | solution.py:53
  81.1 2.6 %weight.1 = (f32[128,1024]{1,0:T(8,128)S(1)}, f32[128,1024]{1,0:T(8,128)S(1)}, f32[1,128]{1,0:T(1,128)S(1)}, f32[264,1024]{1,0:T(8,128)S(1)}) custom-call(s32[4]{0:T(128)S(1)} %get-tuple-element.44.place, bf16[128,2048]{1,0:T(8,128)(2,1)} %get-tuple-element.34.refs_0_, bf16[128,2048]{1,0:T(8,128)(2,1)S(1)} %collective-permute-done.9.refs_1_, ...), custom_call_target="tpu_custom_call" | custom-call | flops 2147483648 | bytes 67108864 | tf_op jit(solution)/shard_map/weight/pallas_call | solution.py:39
  83.8 5.9 %collective-permute-start.19 = (f32[264,1024]{1,0:T(8,128)S(1)}, f32[264,1024]{1,0:T(8,128)S(1)}, u32[]{:S(2)}, u32[]{:S(2)}) collective-permute-start(f32[264,1024]{1,0:T(8,128)S(1)} %get-tuple-element.55), channel_id=1, source_target_pairs={{0,16},{16,0},{32,48},{48,32},{64,80},{80,64},{96,112},{112,96},{1... | collective-permute-start | bytes 3244040 | tf_op jit(solution)/shard_map/ppermute | solution.py:63
  89.7 2.3 %collective-permute-done.19.got = f32[264,1024]{1,0:T(8,128)S(1)} collective-permute-done((f32[264,1024]{1,0:T(8,128)S(1)}, f32[264,1024]{1,0:T(8,128)S(1)}, u32[]{:S(2)}, u32[]{:S(2)}) %collective-permute-start.19) | collective-permute-done | bytes 1081376 | tf_op jit(solution)/shard_map/ppermute | solution.py:63
  (48 shorter events, 11.6 us)
Async XLA Ops:
  2.3 15.8 %collective-permute-start.2 = (bf16[32,2048]{1,0:T(8,128)(2,1)S(1)}, bf16[32,2048]{1,0:T(8,128)(2,1)S(1)}, u32[]{:S(2)}, u32[]{:S(2)}) collective-permute-start(bf16[32,2048]{1,0:T(8,128)(2,1)S(1)} %or_select_fusion.b0), channel_id=1, source_target_pairs={{0,3},{1,0},{2,1},{3,2},{4,7},{5,4},{6,5},{7,6},{8,11},{9,8},{10,9... | collective-permute-start | bytes 393224 | tf_op jit(solution)/shard_map/ppermute | solution.py:53
  9.2 11.1 %collective-permute-start.1 = (bf16[32,2048]{1,0:T(8,128)(2,1)S(1)}, bf16[32,2048]{1,0:T(8,128)(2,1)S(1)}, u32[]{:S(2)}, u32[]{:S(2)}) collective-permute-start(bf16[32,2048]{1,0:T(8,128)(2,1)S(1)} %or_select_fusion.b0), channel_id=1, source_target_pairs={{0,2},{1,3},{2,0},{3,1},{4,6},{5,7},{6,4},{7,5},{8,10},{9,11},{10,... | collective-permute-start | bytes 393224 | tf_op jit(solution)/shard_map/ppermute | solution.py:53
  10.2 10.3 %collective-permute-start = (bf16[32,2048]{1,0:T(8,128)(2,1)S(1)}, bf16[32,2048]{1,0:T(8,128)(2,1)S(1)}, u32[]{:S(2)}, u32[]{:S(2)}) collective-permute-start(bf16[32,2048]{1,0:T(8,128)(2,1)S(1)} %or_select_fusion.b0), channel_id=1, source_target_pairs={{0,1},{1,2},{2,3},{3,0},{4,5},{5,6},{6,7},{7,4},{8,9},{9,10},{10,1... | collective-permute-start | bytes 393224 | tf_op jit(solution)/shard_map/ppermute | solution.py:53
  16.9 3.6 %copy-start.4 = (bf16[2048,1024]{1,0:T(8,128)(2,1)S(1)}, bf16[2048,1024]{1,0:T(8,128)(2,1)}, u32[]{:S(2)}) copy-start(bf16[2048,1024]{1,0:T(8,128)(2,1)} %down.3) | copy-start | bytes 12582916
  18.1 22.2 %copy-start.5 = (f32[2048]{0:T(1024)S(1)}, f32[2048]{0:T(1024)}, u32[]{:S(2)}) copy-start(f32[2048]{0:T(1024)} %param.8) | copy-start | bytes 24580
  24.2 16.1 %all-to-all-start = ((bf16[4,64,2048]{2,1,0:T(8,128)(2,1)}), bf16[4,64,2048]{2,1,0:T(8,128)(2,1)S(1)}, u32[]{:S(2)}, u32[]{:S(2)}) async-start(bf16[4,64,2048]{2,1,0:T(8,128)(2,1)} %get-tuple-element.36), calls=%async_computation | async-start | bytes 2097152 | tf_op jit(solution)/shard_map/all_to_all | solution.py:236
  28.4 14.0 %collective-permute-start.3 = (bf16[128,2048]{1,0:T(8,128)(2,1)}, bf16[128,2048]{1,0:T(8,128)(2,1)}, u32[]{:S(2)}, u32[]{:S(2)}) collective-permute-start(bf16[128,2048]{1,0:T(8,128)(2,1)} %get-tuple-element.34.refs_0_), channel_id=1, source_target_pairs={{0,128},{16,144},{32,160},{48,176},{64,192},{80,208},{96,224},{112... | collective-permute-start | bytes 1572872 | tf_op jit(solution)/shard_map/ppermute | solution.py:63
  31.6 22.3 %collective-permute-start.10 = (bf16[128,2048]{1,0:T(8,128)(2,1)}, bf16[128,2048]{1,0:T(8,128)(2,1)S(1)}, u32[]{:S(2)}, u32[]{:S(2)}) collective-permute-start(bf16[128,2048]{1,0:T(8,128)(2,1)} %get-tuple-element.34.refs_0_), channel_id=1, source_target_pairs={{0,96},{16,112},{32,0},{48,16},{64,32},{80,48},{96,64},{112,80},{1... | collective-permute-start | bytes 1572872 | tf_op jit(solution)/shard_map/ppermute | solution.py:63
  34.0 21.1 %collective-permute-start.9 = (bf16[128,2048]{1,0:T(8,128)(2,1)}, bf16[128,2048]{1,0:T(8,128)(2,1)S(1)}, u32[]{:S(2)}, u32[]{:S(2)}) collective-permute-start(bf16[128,2048]{1,0:T(8,128)(2,1)} %get-tuple-element.34.refs_0_), channel_id=1, source_target_pairs={{0,32},{16,48},{32,64},{48,80},{64,96},{80,112},{96,0},{112,16},{1... | collective-permute-start | bytes 1572872 | tf_op jit(solution)/shard_map/ppermute | solution.py:63
  42.5 18.5 %collective-permute-start.5 = (bf16[128,2048]{1,0:T(8,128)(2,1)}, bf16[128,2048]{1,0:T(8,128)(2,1)S(1)}, u32[]{:S(2)}, u32[]{:S(2)}) collective-permute-start(bf16[128,2048]{1,0:T(8,128)(2,1)} %collective-permute-done.3.refs_3_), channel_id=1, source_target_pairs={{0,96},{16,112},{32,0},{48,16},{64,32},{80,48},{96,64},{112,80},{1... | collective-permute-start | bytes 1572872 | tf_op jit(solution)/shard_map/ppermute | solution.py:63
  44.9 16.0 %collective-permute-start.4 = (bf16[128,2048]{1,0:T(8,128)(2,1)}, bf16[128,2048]{1,0:T(8,128)(2,1)S(1)}, u32[]{:S(2)}, u32[]{:S(2)}) collective-permute-start(bf16[128,2048]{1,0:T(8,128)(2,1)} %collective-permute-done.3.refs_3_), channel_id=1, source_target_pairs={{0,32},{16,48},{32,64},{48,80},{64,96},{80,112},{96,0},{112,16},{1... | collective-permute-start | bytes 1572872 | tf_op jit(solution)/shard_map/ppermute | solution.py:63
  44.9 16.0 %all-to-all-start.1 = ((bf16[8,64,256]{2,1,0:T(8,128)(2,1)}), bf16[8,64,256]{2,1,0:T(8,128)(2,1)S(1)}, u32[]{:S(2)}, u32[]{:S(2)}) async-start(bf16[8,64,256]{2,1,0:T(8,128)(2,1)} %get-tuple-element.40), calls=%async_computation.1 | async-start | bytes 524288 | tf_op jit(solution)/shard_map/all_to_all | solution.py:257
  53.0 4.1 %collective-permute-start.8 = (bf16[32,2048]{1,0:T(8,128)(2,1)S(1)}, bf16[32,2048]{1,0:T(8,128)(2,1)S(1)}, u32[]{:S(2)}, u32[]{:S(2)}) collective-permute-start(bf16[32,2048]{1,0:T(8,128)(2,1)S(1)} %get-tuple-element.38.g0), channel_id=1, source_target_pairs={{0,12},{4,0},{8,4},{12,8},{1,13},{5,1},{9,5},{13,9},{2,14},{6,2},{... | collective-permute-start | bytes 393224 | tf_op jit(solution)/shard_map/ppermute | solution.py:53
  53.9 5.4 %collective-permute-start.7 = (bf16[32,2048]{1,0:T(8,128)(2,1)S(1)}, bf16[32,2048]{1,0:T(8,128)(2,1)S(1)}, u32[]{:S(2)}, u32[]{:S(2)}) collective-permute-start(bf16[32,2048]{1,0:T(8,128)(2,1)S(1)} %get-tuple-element.38.g0), channel_id=1, source_target_pairs={{0,8},{4,12},{8,0},{12,4},{1,9},{5,13},{9,1},{13,5},{2,10},{6,14},... | collective-permute-start | bytes 393224 | tf_op jit(solution)/shard_map/ppermute | solution.py:53
  55.1 5.8 %collective-permute-start.6 = (bf16[32,2048]{1,0:T(8,128)(2,1)S(1)}, bf16[32,2048]{1,0:T(8,128)(2,1)S(1)}, u32[]{:S(2)}, u32[]{:S(2)}) collective-permute-start(bf16[32,2048]{1,0:T(8,128)(2,1)S(1)} %get-tuple-element.38.g0), channel_id=1, source_target_pairs={{0,4},{4,8},{8,12},{12,0},{1,5},{5,9},{9,13},{13,1},{2,6},{6,10},{... | collective-permute-start | bytes 393224 | tf_op jit(solution)/shard_map/ppermute | solution.py:53
  61.0 20.1 %collective-permute-start.12 = (bf16[128,2048]{1,0:T(8,128)(2,1)S(1)}, bf16[128,2048]{1,0:T(8,128)(2,1)S(1)}, u32[]{:S(2)}, u32[]{:S(2)}) collective-permute-start(bf16[128,2048]{1,0:T(8,128)(2,1)S(1)} %pad_maximum_fusion.1), channel_id=1, source_target_pairs={{0,96},{16,112},{32,0},{48,16},{64,32},{80,48},{96,64},{112,80},{1... | collective-permute-start | bytes 1572872 | tf_op jit(solution)/shard_map/ppermute | solution.py:63
  63.7 17.4 %collective-permute-start.11 = (bf16[128,2048]{1,0:T(8,128)(2,1)S(1)}, bf16[128,2048]{1,0:T(8,128)(2,1)S(1)}, u32[]{:S(2)}, u32[]{:S(2)}) collective-permute-start(bf16[128,2048]{1,0:T(8,128)(2,1)S(1)} %pad_maximum_fusion), channel_id=1, source_target_pairs={{0,32},{16,48},{32,64},{48,80},{64,96},{80,112},{96,0},{112,16},{1... | collective-permute-start | bytes 1572872 | tf_op jit(solution)/shard_map/ppermute | solution.py:63
  63.8 7.0 %collective-permute-start.15 = (bf16[8,64,256]{2,1,0:T(8,128)(2,1)S(1)}, bf16[8,64,256]{2,1,0:T(8,128)(2,1)S(1)}, u32[]{:S(2)}, u32[]{:S(2)}) collective-permute-start(bf16[8,64,256]{2,1,0:T(8,128)(2,1)S(1)} %all-to-all-done.1.refs_8_), channel_id=1, source_target_pairs={{0,12},{4,0},{8,4},{12,8},{1,13},{5,1},{9,5},{13,9},{2,14},{6,2},{... | collective-permute-start | bytes 786440 | tf_op jit(solution)/shard_map/ppermute | solution.py:53
  64.5 10.4 %collective-permute-start.14 = (bf16[8,64,256]{2,1,0:T(8,128)(2,1)S(1)}, bf16[8,64,256]{2,1,0:T(8,128)(2,1)S(1)}, u32[]{:S(2)}, u32[]{:S(2)}) collective-permute-start(bf16[8,64,256]{2,1,0:T(8,128)(2,1)S(1)} %all-to-all-done.1.refs_8_), channel_id=1, source_target_pairs={{0,8},{4,12},{8,0},{12,4},{1,9},{5,13},{9,1},{13,5},{2,10},{6,14},... | collective-permute-start | bytes 786440 | tf_op jit(solution)/shard_map/ppermute | solution.py:53
  66.0 11.4 %collective-permute-start.13 = (bf16[8,64,256]{2,1,0:T(8,128)(2,1)S(1)}, bf16[8,64,256]{2,1,0:T(8,128)(2,1)S(1)}, u32[]{:S(2)}, u32[]{:S(2)}) collective-permute-start(bf16[8,64,256]{2,1,0:T(8,128)(2,1)S(1)} %all-to-all-done.1.refs_8_), channel_id=1, source_target_pairs={{0,4},{4,8},{8,12},{12,0},{1,5},{5,9},{9,13},{13,1},{2,6},{6,10},{... | collective-permute-start | bytes 786440 | tf_op jit(solution)/shard_map/ppermute | solution.py:53
  70.9 12.9 %collective-permute-start.16 = (bf16[32,1024]{1,0:T(8,128)(2,1)S(1)}, bf16[32,1024]{1,0:T(8,128)(2,1)S(1)}, u32[]{:S(2)}, u32[]{:S(2)}) collective-permute-start(bf16[32,1024]{1,0:T(8,128)(2,1)S(1)} %get-tuple-element.52), channel_id=1, source_target_pairs={{0,3},{1,0},{2,1},{3,2},{4,7},{5,4},{6,5},{7,6},{8,11},{9,8},{10,9... | collective-permute-start | bytes 196616 | tf_op jit(solution)/shard_map/ppermute | solution.py:53
  74.9 8.9 %collective-permute-start.17 = (bf16[32,1024]{1,0:T(8,128)(2,1)S(1)}, bf16[32,1024]{1,0:T(8,128)(2,1)S(1)}, u32[]{:S(2)}, u32[]{:S(2)}) collective-permute-start(bf16[32,1024]{1,0:T(8,128)(2,1)S(1)} %get-tuple-element.53), channel_id=1, source_target_pairs={{0,2},{1,3},{2,0},{3,1},{4,6},{5,7},{6,4},{7,5},{8,10},{9,11},{10,... | collective-permute-start | bytes 196616 | tf_op jit(solution)/shard_map/ppermute | solution.py:53
  77.4 6.4 %collective-permute-start.18 = (bf16[32,1024]{1,0:T(8,128)(2,1)S(1)}, bf16[32,1024]{1,0:T(8,128)(2,1)S(1)}, u32[]{:S(2)}, u32[]{:S(2)}) collective-permute-start(bf16[32,1024]{1,0:T(8,128)(2,1)S(1)} %get-tuple-element.54), channel_id=1, source_target_pairs={{0,1},{1,2},{2,3},{3,0},{4,5},{5,6},{6,7},{7,4},{8,9},{9,10},{10,1... | collective-permute-start | bytes 196616 | tf_op jit(solution)/shard_map/ppermute | solution.py:53
  83.8 8.2 %collective-permute-start.19 = (f32[264,1024]{1,0:T(8,128)S(1)}, f32[264,1024]{1,0:T(8,128)S(1)}, u32[]{:S(2)}, u32[]{:S(2)}) collective-permute-start(f32[264,1024]{1,0:T(8,128)S(1)} %get-tuple-element.55), channel_id=1, source_target_pairs={{0,16},{16,0},{32,48},{48,32},{64,80},{80,64},{96,112},{112,96},{1... | collective-permute-start | bytes 3244040 | tf_op jit(solution)/shard_map/ppermute | solution.py:63
  (4 other events, 10.1 us)

commit v4 on v3

--- a/solution.py
+++ b/solution.py
@@ -134,8 +134,8 @@
 
 def weight_kernel(place, *refs):
     pieces, pairs = refs[:8], refs[8:12]
-    up_keep, down_keep, bias_keep, send = refs[12:16]
-    act_s, grad_s = refs[16:18]
+    up_keep, down_keep, bias_keep, up_send, down_send = refs[12:17]
+    act_s, grad_s = refs[17:19]
     row, x, z, core = place[0], place[1], place[2], place[3]
     whole = pieces[0].shape[0]
     rows = whole // SIDE
@@ -157,14 +157,14 @@
     narrow, width = up_keep.shape
     own = pl.multiple_of(core * narrow, narrow)
     other = pl.multiple_of((1 - core) * narrow, narrow)
-    send[2 * narrow :, :] = jnp.zeros((send.shape[0] - 2 * narrow, width), f32)
-    for at, out, i in ((own, bias_keep, 0), (other, send, 2 * narrow)):
+    up_send[narrow:, :] = jnp.zeros((up_send.shape[0] - narrow, width), f32)
+    for at, out, i in ((own, bias_keep, 0), (other, up_send, narrow)):
         total = jnp.sum(grad_s[:, pl.ds(at, narrow)].astype(f32), axis=0, keepdims=True)
         out[i : i + 1, :narrow] = total
     tile = 256
-    for scratch, offset, keep, to in (
-        (grad_s, 0, up_keep, 0),
-        (act_s, width, down_keep, narrow),
+    for scratch, offset, keep, send in (
+        (grad_s, 0, up_keep, up_send),
+        (act_s, width, down_keep, down_send),
     ):
         left = jnp.concatenate(
             [scratch[:, pl.ds(own, narrow)].T, scratch[:, pl.ds(other, narrow)].T], axis=0
@@ -178,17 +178,19 @@
                 term = dot(left[:, q * 2 * whole : (q + 1) * 2 * whole], right, ((1,), (0,)))
                 acc = term if acc is None else acc + term
             keep[:, at] = acc[:narrow]
-            send[to : to + narrow, at] = acc[narrow:]
-
-
-def last_kernel(up_keep, down_keep, bias_keep, got, keep, i1, i2, i3, up, down, bias, inp):
+            send[:narrow, at] = acc[narrow:]
+
+
+def last_kernel(
+    up_keep, down_keep, bias_keep, up_got, down_got, keep, i1, i2, i3, up, down, bias, inp
+):
     inp[...] = (
         keep[...] + i1[...].astype(f32) + i2[...].astype(f32) + i3[...].astype(f32)
     ).astype(bf16)
     narrow = up_keep.shape[0]
-    up[...] = (up_keep[...] + got[:narrow, :]).T
-    down[...] = down_keep[...] + got[narrow : 2 * narrow, :]
-    bias[...] = bias_keep[...] + got[2 * narrow : 2 * narrow + 1, :narrow]
+    up[...] = (up_keep[...] + up_got[:narrow, :]).T
+    down[...] = down_keep[...] + down_got[...]
+    bias[...] = bias_keep[...] + up_got[narrow : narrow + 1, :narrow]
 
 
 def local(tokens, up_weight, up_bias, down_weight, out_grad, bucket_lengths):
@@ -287,9 +289,9 @@
 
     block, line = shape((narrow, width), f32), shape((1, narrow), f32)
     count = PEERS * SIDE * rows
-    up_keep, down_keep, bias_keep, send = call(
+    up_keep, down_keep, bias_keep, up_send, down_send = call(
         weight_kernel,
-        (block, block, line, shape((2 * narrow + 8, width), f32)),
+        (block, block, line, shape((narrow + 8, width), f32), block),
         [pltpu.VMEM((count, NC * narrow), bf16)] * 2,
         (8 * count * width * narrow * NC, WEIGHT << 20),
         place,
@@ -301,7 +303,7 @@
         smem=1,
         name="weight",
     )
-    send, i1, i2, i3 = lax.optimization_barrier((send, i1, i2, i3))
+    down_send, i1, i2, i3 = lax.optimization_barrier((down_send, i1, i2, i3))
     up_grad, down_grad, bias_grad, input_grad = call(
         last_kernel,
         (shape((width, narrow), f32), block, line, shape((rows, width), bf16)),
@@ -310,7 +312,8 @@
         up_keep,
         down_keep,
         bias_keep,
-        flip_core(send),
+        flip_core(up_send),
+        flip_core(down_send),
         keep,
         i1,
         i2,

time: 93.6 us -> 92.8 us (level)
    ppermute x8 -> x9, waiting for transfers between devices: 3.01 us -> 2.22 us  [move(): return lax.ppermute(array, 'dp', pairs)]
    ppermute x8 -> x9, starting transfers between devices: 16.6 us -> 16.7 us  [move(): return lax.ppermute(array, 'dp', pairs)]
  transfers between devices with their start and end apart: 22 -> 23, of which waited for: 8 -> 8; matrix products, arithmetic and copies ran while one was open for 0% -> 0% of each run, Pallas kernels for 8% -> 8%
where the time goes in v4:
time: 92.8 us; the launch traced here: 92.4 us
  starting transfers between devices  53.9 us (58%)
  waiting for transfers between devices  16.7 us (18%)
  Pallas kernels  12.6 us (14%)
  local copies, waits for them, and re-layouts  6.65 us (7%)
  between operations  1.43 us (2%)
  other arithmetic  1.15 us (1%)
    ppermute x12, starting transfers between devices, shift(): lax.ppermute(array, axis, [(i, (i + by) % count) for i in range(count)])  24.9 us
    ppermute x9, starting transfers between devices, move(): return lax.ppermute(array, 'dp', pairs)  16.7 us
    pallas_call x6, Pallas kernels, call(): pl.pallas_call(kernel, out_shape=outs, in_specs=[SMEM] * smem + [VMEM] *...  12.6 us
    ppermute x12, waiting for transfers between devices, shift(): lax.ppermute(array, axis, [(i, (i + by) % count) for i in range(count)])  8.19 us
    all_to_all x1, starting transfers between devices, local(): pair = lax.all_to_all(pair, 'dp', 0, 0, axis_index_groups=groups)  8.08 us
    unnamed x12, local copies, waits for them, and re-layouts  6.58 us
    all_to_all x1, waiting for transfers between devices, local(): got = lax.all_to_all(send, 'row', 0, 0)  6.24 us
    all_to_all x1, starting transfers between devices, local(): got = lax.all_to_all(send, 'row', 0, 0)  4.26 us
  transfers between devices with their start and end apart: 23, of which 8 were waited for; matrix products, arithmetic and copies ran while one was open for 0% of the time, Pallas kernels for 8%

profile of v4, /device:TPU:1, one launch (start us, length us, event | category | flops | bytes accessed | tf_op | source)
XLA Modules:
  0.0 92.4 jit_solution(16078141190709322672)
XLA Ops:
  2.3 6.9 %collective-permute-start.2 = (bf16[32,2048]{1,0:T(8,128)(2,1)S(1)}, bf16[32,2048]{1,0:T(8,128)(2,1)S(1)}, u32[]{:S(2)}, u32[]{:S(2)}) collective-permute-start(bf16[32,2048]{1,0:T(8,128)(2,1)S(1)} %or_select_fusion.b0), channel_id=1, source_target_pairs={{0,3},{1,0},{2,1},{3,2},{4,7},{5,4},{6,5},{7,6},{8,11},{9,8},{10,9... | collective-permute-start | bytes 393224 | tf_op jit(solution)/shard_map/ppermute | solution.py:53
  10.2 2.3 %collective-permute-start = (bf16[32,2048]{1,0:T(8,128)(2,1)S(1)}, bf16[32,2048]{1,0:T(8,128)(2,1)S(1)}, u32[]{:S(2)}, u32[]{:S(2)}) collective-permute-start(bf16[32,2048]{1,0:T(8,128)(2,1)S(1)} %or_select_fusion.b0), channel_id=1, source_target_pairs={{0,1},{1,2},{2,3},{3,0},{4,5},{5,6},{6,7},{7,4},{8,9},{9,10},{10,1... | collective-permute-start | bytes 393224 | tf_op jit(solution)/shard_map/ppermute | solution.py:53
  12.5 2.2 %copy-done = bf16[1024,2048]{1,0:T(8,128)(2,1)S(1)} copy-done((bf16[1024,2048]{1,0:T(8,128)(2,1)S(1)}, bf16[1024,2048]{1,0:T(8,128)(2,1)}, u32[]{:S(2)}) %copy-start) | copy-done | bytes 4194328
  14.7 2.2 %copy-done.3 = bf16[2048,1024]{1,0:T(8,128)(2,1)S(1)} copy-done((bf16[2048,1024]{1,0:T(8,128)(2,1)S(1)}, bf16[2048,1024]{1,0:T(8,128)(2,1)}, u32[]{:S(2)}) %copy-start.3) | copy-done | bytes 4194328
  18.1 2.2 %collective-permute-done.1.b2 = bf16[32,2048]{1,0:T(8,128)(2,1)S(1)} collective-permute-done((bf16[32,2048]{1,0:T(8,128)(2,1)S(1)}, bf16[32,2048]{1,0:T(8,128)(2,1)S(1)}, u32[]{:S(2)}, u32[]{:S(2)}) %collective-permute-start.1) | collective-permute-done | bytes 131104 | tf_op jit(solution)/shard_map/ppermute | solution.py:53
  20.5 3.7 %first.1 = (bf16[128,2048]{1,0:T(8,128)(2,1)}, f32[64,2048]{1,0:T(8,128)S(1)}, bf16[4,64,2048]{2,1,0:T(8,128)(2,1)}) custom-call(s32[4]{0:T(128)S(1)} %near.1.place, bf16[32,2048]{1,0:T(8,128)(2,1)S(1)} %or_select_fusion.b0, bf16[32,2048]{1,0:T(8,128)(2,1)S(1)} %collective-permute-done.b1, bf16[32,2048]{1,0:T(8,128)(2,1)S(1)} %collective-permute-done.1.b2, ...), custom_call_target="tpu_custom_call" | custom-call | flops 2147483648 | bytes 8388608 | tf_op jit(solution)/shard_map/first/pallas_call | solution.py:39
  24.2 4.3 %all-to-all-start = ((bf16[4,64,2048]{2,1,0:T(8,128)(2,1)}), bf16[4,64,2048]{2,1,0:T(8,128)(2,1)S(1)}, u32[]{:S(2)}, u32[]{:S(2)}) async-start(bf16[4,64,2048]{2,1,0:T(8,128)(2,1)} %get-tuple-element.37), calls=%async_computation | async-start | bytes 2097152 | tf_op jit(solution)/shard_map/all_to_all | solution.py:238
  28.4 3.1 %collective-permute-start.3 = (bf16[128,2048]{1,0:T(8,128)(2,1)}, bf16[128,2048]{1,0:T(8,128)(2,1)}, u32[]{:S(2)}, u32[]{:S(2)}) collective-permute-start(bf16[128,2048]{1,0:T(8,128)(2,1)} %get-tuple-element.35.refs_0_), channel_id=1, source_target_pairs={{0,128},{16,144},{32,160},{48,176},{64,192},{80,208},{96,224},{112... | collective-permute-start | bytes 1572872 | tf_op jit(solution)/shard_map/ppermute | solution.py:63
  31.6 2.5 %collective-permute-start.10 = (bf16[128,2048]{1,0:T(8,128)(2,1)}, bf16[128,2048]{1,0:T(8,128)(2,1)S(1)}, u32[]{:S(2)}, u32[]{:S(2)}) collective-permute-start(bf16[128,2048]{1,0:T(8,128)(2,1)} %get-tuple-element.35.refs_0_), channel_id=1, source_target_pairs={{0,96},{16,112},{32,0},{48,16},{64,32},{80,48},{96,64},{112,80},{1... | collective-permute-start | bytes 1572872 | tf_op jit(solution)/shard_map/ppermute | solution.py:63
  34.0 6.2 %all-to-all-done.got = bf16[4,64,2048]{2,1,0:T(8,128)(2,1)S(1)} async-done(((bf16[4,64,2048]{2,1,0:T(8,128)(2,1)}), bf16[4,64,2048]{2,1,0:T(8,128)(2,1)S(1)}, u32[]{:S(2)}, u32[]{:S(2)}) %all-to-all-start) | async-done | bytes 1048608 | tf_op jit(solution)/shard_map/all_to_all | solution.py:238
  42.5 2.4 %collective-permute-start.5 = (bf16[128,2048]{1,0:T(8,128)(2,1)}, bf16[128,2048]{1,0:T(8,128)(2,1)S(1)}, u32[]{:S(2)}, u32[]{:S(2)}) collective-permute-start(bf16[128,2048]{1,0:T(8,128)(2,1)} %collective-permute-done.3.refs_3_), channel_id=1, source_target_pairs={{0,96},{16,112},{32,0},{48,16},{64,32},{80,48},{96,64},{112,80},{1... | collective-permute-start | bytes 1572872 | tf_op jit(solution)/shard_map/ppermute | solution.py:63
  44.9 8.1 %all-to-all-start.1 = ((bf16[8,64,256]{2,1,0:T(8,128)(2,1)}), bf16[8,64,256]{2,1,0:T(8,128)(2,1)S(1)}, u32[]{:S(2)}, u32[]{:S(2)}) async-start(bf16[8,64,256]{2,1,0:T(8,128)(2,1)} %get-tuple-element.41), calls=%async_computation.1 | async-start | bytes 524288 | tf_op jit(solution)/shard_map/all_to_all | solution.py:259
  55.1 2.0 %collective-permute-done.8.g3 = bf16[32,2048]{1,0:T(8,128)(2,1)S(1)} collective-permute-done((bf16[32,2048]{1,0:T(8,128)(2,1)S(1)}, bf16[32,2048]{1,0:T(8,128)(2,1)S(1)}, u32[]{:S(2)}, u32[]{:S(2)}) %collective-permute-start.8) | collective-permute-done | bytes 131104 | tf_op jit(solution)/shard_map/ppermute | solution.py:53
  57.1 2.2 %collective-permute-done.7.g2 = bf16[32,2048]{1,0:T(8,128)(2,1)S(1)} collective-permute-done((bf16[32,2048]{1,0:T(8,128)(2,1)S(1)}, bf16[32,2048]{1,0:T(8,128)(2,1)S(1)}, u32[]{:S(2)}, u32[]{:S(2)}) %collective-permute-start.7) | collective-permute-done | bytes 131104 | tf_op jit(solution)/shard_map/ppermute | solution.py:53
  59.3 1.6 %collective-permute-done.6.g1 = bf16[32,2048]{1,0:T(8,128)(2,1)S(1)} collective-permute-done((bf16[32,2048]{1,0:T(8,128)(2,1)S(1)}, bf16[32,2048]{1,0:T(8,128)(2,1)S(1)}, u32[]{:S(2)}, u32[]{:S(2)}) %collective-permute-start.6) | collective-permute-done | bytes 131104 | tf_op jit(solution)/shard_map/ppermute | solution.py:53
  61.0 2.7 %collective-permute-start.12 = (bf16[128,2048]{1,0:T(8,128)(2,1)S(1)}, bf16[128,2048]{1,0:T(8,128)(2,1)S(1)}, u32[]{:S(2)}, u32[]{:S(2)}) collective-permute-start(bf16[128,2048]{1,0:T(8,128)(2,1)S(1)} %pad_maximum_fusion.1), channel_id=1, source_target_pairs={{0,96},{16,112},{32,0},{48,16},{64,32},{80,48},{96,64},{112,80},{1... | collective-permute-start | bytes 1572872 | tf_op jit(solution)/shard_map/ppermute | solution.py:63
  66.2 2.2 %copy-done.2 = bf16[1024,2048]{1,0:T(8,128)(2,1)S(1)} copy-done((bf16[1024,2048]{1,0:T(8,128)(2,1)S(1)}, bf16[1024,2048]{1,0:T(8,128)(2,1)}, u32[]{:S(2)}) %copy-start.2) | copy-done | bytes 4194328
  68.4 2.5 %input.1 = (f32[32,1024]{1,0:T(8,128)S(1)}, bf16[32,1024]{1,0:T(8,128)(2,1)S(1)}, bf16[32,1024]{1,0:T(8,128)(2,1)S(1)}, bf16[32,1024]{1,0:T(8,128)(2,1)S(1)}, s32[4]{0:T(128)S(1)}) custom-call(s32[4]{0:T(128)S(1)} %near.1.place, bf16[32,2048]{1,0:T(8,128)(2,1)S(1)} %get-tuple-element.39.g0, bf16[32,2048]{1,0:T(8,128)(2,1)S(1)} %collective-permute-done.6.g1, ...), custom_call_target="tpu_custom_call" | custom-call | flops 536870912 | bytes 67108864 | tf_op jit(solution)/shard_map/input/pallas_call | solution.py:39
  70.9 4.0 %collective-permute-start.17 = (bf16[32,1024]{1,0:T(8,128)(2,1)S(1)}, bf16[32,1024]{1,0:T(8,128)(2,1)S(1)}, u32[]{:S(2)}, u32[]{:S(2)}) collective-permute-start(bf16[32,1024]{1,0:T(8,128)(2,1)S(1)} %get-tuple-element.54), channel_id=1, source_target_pairs={{0,3},{1,0},{2,1},{3,2},{4,7},{5,4},{6,5},{7,6},{8,11},{9,8},{10,9... | collective-permute-start | bytes 196616 | tf_op jit(solution)/shard_map/ppermute | solution.py:53
  74.9 2.5 %collective-permute-start.18 = (bf16[32,1024]{1,0:T(8,128)(2,1)S(1)}, bf16[32,1024]{1,0:T(8,128)(2,1)S(1)}, u32[]{:S(2)}, u32[]{:S(2)}) collective-permute-start(bf16[32,1024]{1,0:T(8,128)(2,1)S(1)} %get-tuple-element.55), channel_id=1, source_target_pairs={{0,2},{1,3},{2,0},{3,1},{4,6},{5,7},{6,4},{7,5},{8,10},{9,11},{10,... | collective-permute-start | bytes 196616 | tf_op jit(solution)/shard_map/ppermute | solution.py:53
  77.4 3.7 %collective-permute-start.19 = (bf16[32,1024]{1,0:T(8,128)(2,1)S(1)}, bf16[32,1024]{1,0:T(8,128)(2,1)S(1)}, u32[]{:S(2)}, u32[]{:S(2)}) collective-permute-start(bf16[32,1024]{1,0:T(8,128)(2,1)S(1)} %get-tuple-element.56), channel_id=1, source_target_pairs={{0,1},{1,2},{2,3},{3,0},{4,5},{5,6},{6,7},{7,4},{8,9},{9,10},{10,1... | collective-permute-start | bytes 196616 | tf_op jit(solution)/shard_map/ppermute | solution.py:53
  81.1 2.6 %weight.1 = (f32[128,1024]{1,0:T(8,128)S(1)}, f32[128,1024]{1,0:T(8,128)S(1)}, f32[1,128]{1,0:T(1,128)S(1)}, f32[136,1024]{1,0:T(8,128)S(1)}, f32[128,1024]{1,0:T(8,128)S(1)}) custom-call(s32[4]{0:T(128)S(1)} %get-tuple-element.45.place, bf16[128,2048]{1,0:T(8,128)(2,1)} %get-tuple-element.35.refs_0_, bf16[128,2048]{1,0:T(8,128)(2,1)S(1)} %collective-permute-done.9.refs_1_, ...), custom_call_target="tpu_custom_call" | custom-call | flops 2147483648 | bytes 67108864 | tf_op jit(solution)/shard_map/weight/pallas_call | solution.py:39
  83.8 4.0 %collective-permute-start.16 = (f32[136,1024]{1,0:T(8,128)S(1)}, f32[136,1024]{1,0:T(8,128)S(1)}, u32[]{:S(2)}, u32[]{:S(2)}) collective-permute-start(f32[136,1024]{1,0:T(8,128)S(1)} %get-tuple-element.52), channel_id=1, source_target_pairs={{0,16},{16,0},{32,48},{48,32},{64,80},{80,64},{96,112},{112,96},{1... | collective-permute-start | bytes 1671176 | tf_op jit(solution)/shard_map/ppermute | solution.py:63
  87.8 1.9 %collective-permute-start.20 = (f32[128,1024]{1,0:T(8,128)S(1)}, f32[128,1024]{1,0:T(8,128)S(1)}, u32[]{:S(2)}, u32[]{:S(2)}) collective-permute-start(f32[128,1024]{1,0:T(8,128)S(1)} %get-tuple-element.57), channel_id=1, source_target_pairs={{0,16},{16,0},{32,48},{48,32},{64,80},{80,64},{96,112},{112,96},{1... | collective-permute-start | bytes 1572872 | tf_op jit(solution)/shard_map/ppermute | solution.py:63
  (50 shorter events, 13.1 us)
Async XLA Ops:
  2.3 15.8 %collective-permute-start.2 = (bf16[32,2048]{1,0:T(8,128)(2,1)S(1)}, bf16[32,2048]{1,0:T(8,128)(2,1)S(1)}, u32[]{:S(2)}, u32[]{:S(2)}) collective-permute-start(bf16[32,2048]{1,0:T(8,128)(2,1)S(1)} %or_select_fusion.b0), channel_id=1, source_target_pairs={{0,3},{1,0},{2,1},{3,2},{4,7},{5,4},{6,5},{7,6},{8,11},{9,8},{10,9... | collective-permute-start | bytes 393224 | tf_op jit(solution)/shard_map/ppermute | solution.py:53
  9.2 11.1 %collective-permute-start.1 = (bf16[32,2048]{1,0:T(8,128)(2,1)S(1)}, bf16[32,2048]{1,0:T(8,128)(2,1)S(1)}, u32[]{:S(2)}, u32[]{:S(2)}) collective-permute-start(bf16[32,2048]{1,0:T(8,128)(2,1)S(1)} %or_select_fusion.b0), channel_id=1, source_target_pairs={{0,2},{1,3},{2,0},{3,1},{4,6},{5,7},{6,4},{7,5},{8,10},{9,11},{10,... | collective-permute-start | bytes 393224 | tf_op jit(solution)/shard_map/ppermute | solution.py:53
  10.2 10.3 %collective-permute-start = (bf16[32,2048]{1,0:T(8,128)(2,1)S(1)}, bf16[32,2048]{1,0:T(8,128)(2,1)S(1)}, u32[]{:S(2)}, u32[]{:S(2)}) collective-permute-start(bf16[32,2048]{1,0:T(8,128)(2,1)S(1)} %or_select_fusion.b0), channel_id=1, source_target_pairs={{0,1},{1,2},{2,3},{3,0},{4,5},{5,6},{6,7},{7,4},{8,9},{9,10},{10,1... | collective-permute-start | bytes 393224 | tf_op jit(solution)/shard_map/ppermute | solution.py:53
  18.1 22.2 %copy-start.5 = (f32[2048]{0:T(1024)S(1)}, f32[2048]{0:T(1024)}, u32[]{:S(2)}) copy-start(f32[2048]{0:T(1024)} %param.8) | copy-start | bytes 24580
  24.2 16.1 %all-to-all-start = ((bf16[4,64,2048]{2,1,0:T(8,128)(2,1)}), bf16[4,64,2048]{2,1,0:T(8,128)(2,1)S(1)}, u32[]{:S(2)}, u32[]{:S(2)}) async-start(bf16[4,64,2048]{2,1,0:T(8,128)(2,1)} %get-tuple-element.37), calls=%async_computation | async-start | bytes 2097152 | tf_op jit(solution)/shard_map/all_to_all | solution.py:238
  28.4 14.0 %collective-permute-start.3 = (bf16[128,2048]{1,0:T(8,128)(2,1)}, bf16[128,2048]{1,0:T(8,128)(2,1)}, u32[]{:S(2)}, u32[]{:S(2)}) collective-permute-start(bf16[128,2048]{1,0:T(8,128)(2,1)} %get-tuple-element.35.refs_0_), channel_id=1, source_target_pairs={{0,128},{16,144},{32,160},{48,176},{64,192},{80,208},{96,224},{112... | collective-permute-start | bytes 1572872 | tf_op jit(solution)/shard_map/ppermute | solution.py:63
  31.6 22.3 %collective-permute-start.10 = (bf16[128,2048]{1,0:T(8,128)(2,1)}, bf16[128,2048]{1,0:T(8,128)(2,1)S(1)}, u32[]{:S(2)}, u32[]{:S(2)}) collective-permute-start(bf16[128,2048]{1,0:T(8,128)(2,1)} %get-tuple-element.35.refs_0_), channel_id=1, source_target_pairs={{0,96},{16,112},{32,0},{48,16},{64,32},{80,48},{96,64},{112,80},{1... | collective-permute-start | bytes 1572872 | tf_op jit(solution)/shard_map/ppermute | solution.py:63
  34.0 21.1 %collective-permute-start.9 = (bf16[128,2048]{1,0:T(8,128)(2,1)}, bf16[128,2048]{1,0:T(8,128)(2,1)S(1)}, u32[]{:S(2)}, u32[]{:S(2)}) collective-permute-start(bf16[128,2048]{1,0:T(8,128)(2,1)} %get-tuple-element.35.refs_0_), channel_id=1, source_target_pairs={{0,32},{16,48},{32,64},{48,80},{64,96},{80,112},{96,0},{112,16},{1... | collective-permute-start | bytes 1572872 | tf_op jit(solution)/shard_map/ppermute | solution.py:63
  42.5 18.5 %collective-permute-start.5 = (bf16[128,2048]{1,0:T(8,128)(2,1)}, bf16[128,2048]{1,0:T(8,128)(2,1)S(1)}, u32[]{:S(2)}, u32[]{:S(2)}) collective-permute-start(bf16[128,2048]{1,0:T(8,128)(2,1)} %collective-permute-done.3.refs_3_), channel_id=1, source_target_pairs={{0,96},{16,112},{32,0},{48,16},{64,32},{80,48},{96,64},{112,80},{1... | collective-permute-start | bytes 1572872 | tf_op jit(solution)/shard_map/ppermute | solution.py:63
  44.9 16.0 %collective-permute-start.4 = (bf16[128,2048]{1,0:T(8,128)(2,1)}, bf16[128,2048]{1,0:T(8,128)(2,1)S(1)}, u32[]{:S(2)}, u32[]{:S(2)}) collective-permute-start(bf16[128,2048]{1,0:T(8,128)(2,1)} %collective-permute-done.3.refs_3_), channel_id=1, source_target_pairs={{0,32},{16,48},{32,64},{48,80},{64,96},{80,112},{96,0},{112,16},{1... | collective-permute-start | bytes 1572872 | tf_op jit(solution)/shard_map/ppermute | solution.py:63
  44.9 16.0 %all-to-all-start.1 = ((bf16[8,64,256]{2,1,0:T(8,128)(2,1)}), bf16[8,64,256]{2,1,0:T(8,128)(2,1)S(1)}, u32[]{:S(2)}, u32[]{:S(2)}) async-start(bf16[8,64,256]{2,1,0:T(8,128)(2,1)} %get-tuple-element.41), calls=%async_computation.1 | async-start | bytes 524288 | tf_op jit(solution)/shard_map/all_to_all | solution.py:259
  53.0 4.1 %collective-permute-start.8 = (bf16[32,2048]{1,0:T(8,128)(2,1)S(1)}, bf16[32,2048]{1,0:T(8,128)(2,1)S(1)}, u32[]{:S(2)}, u32[]{:S(2)}) collective-permute-start(bf16[32,2048]{1,0:T(8,128)(2,1)S(1)} %get-tuple-element.39.g0), channel_id=1, source_target_pairs={{0,12},{4,0},{8,4},{12,8},{1,13},{5,1},{9,5},{13,9},{2,14},{6,2},{... | collective-permute-start | bytes 393224 | tf_op jit(solution)/shard_map/ppermute | solution.py:53
  53.9 5.4 %collective-permute-start.7 = (bf16[32,2048]{1,0:T(8,128)(2,1)S(1)}, bf16[32,2048]{1,0:T(8,128)(2,1)S(1)}, u32[]{:S(2)}, u32[]{:S(2)}) collective-permute-start(bf16[32,2048]{1,0:T(8,128)(2,1)S(1)} %get-tuple-element.39.g0), channel_id=1, source_target_pairs={{0,8},{4,12},{8,0},{12,4},{1,9},{5,13},{9,1},{13,5},{2,10},{6,14},... | collective-permute-start | bytes 393224 | tf_op jit(solution)/shard_map/ppermute | solution.py:53
  55.1 5.8 %collective-permute-start.6 = (bf16[32,2048]{1,0:T(8,128)(2,1)S(1)}, bf16[32,2048]{1,0:T(8,128)(2,1)S(1)}, u32[]{:S(2)}, u32[]{:S(2)}) collective-permute-start(bf16[32,2048]{1,0:T(8,128)(2,1)S(1)} %get-tuple-element.39.g0), channel_id=1, source_target_pairs={{0,4},{4,8},{8,12},{12,0},{1,5},{5,9},{9,13},{13,1},{2,6},{6,10},{... | collective-permute-start | bytes 393224 | tf_op jit(solution)/shard_map/ppermute | solution.py:53
  61.0 20.1 %collective-permute-start.12 = (bf16[128,2048]{1,0:T(8,128)(2,1)S(1)}, bf16[128,2048]{1,0:T(8,128)(2,1)S(1)}, u32[]{:S(2)}, u32[]{:S(2)}) collective-permute-start(bf16[128,2048]{1,0:T(8,128)(2,1)S(1)} %pad_maximum_fusion.1), channel_id=1, source_target_pairs={{0,96},{16,112},{32,0},{48,16},{64,32},{80,48},{96,64},{112,80},{1... | collective-permute-start | bytes 1572872 | tf_op jit(solution)/shard_map/ppermute | solution.py:63
  63.7 17.4 %collective-permute-start.11 = (bf16[128,2048]{1,0:T(8,128)(2,1)S(1)}, bf16[128,2048]{1,0:T(8,128)(2,1)S(1)}, u32[]{:S(2)}, u32[]{:S(2)}) collective-permute-start(bf16[128,2048]{1,0:T(8,128)(2,1)S(1)} %pad_maximum_fusion), channel_id=1, source_target_pairs={{0,32},{16,48},{32,64},{48,80},{64,96},{80,112},{96,0},{112,16},{1... | collective-permute-start | bytes 1572872 | tf_op jit(solution)/shard_map/ppermute | solution.py:63
  63.8 7.0 %collective-permute-start.15 = (bf16[8,64,256]{2,1,0:T(8,128)(2,1)S(1)}, bf16[8,64,256]{2,1,0:T(8,128)(2,1)S(1)}, u32[]{:S(2)}, u32[]{:S(2)}) collective-permute-start(bf16[8,64,256]{2,1,0:T(8,128)(2,1)S(1)} %all-to-all-done.1.refs_8_), channel_id=1, source_target_pairs={{0,12},{4,0},{8,4},{12,8},{1,13},{5,1},{9,5},{13,9},{2,14},{6,2},{... | collective-permute-start | bytes 786440 | tf_op jit(solution)/shard_map/ppermute | solution.py:53
  64.5 10.4 %collective-permute-start.14 = (bf16[8,64,256]{2,1,0:T(8,128)(2,1)S(1)}, bf16[8,64,256]{2,1,0:T(8,128)(2,1)S(1)}, u32[]{:S(2)}, u32[]{:S(2)}) collective-permute-start(bf16[8,64,256]{2,1,0:T(8,128)(2,1)S(1)} %all-to-all-done.1.refs_8_), channel_id=1, source_target_pairs={{0,8},{4,12},{8,0},{12,4},{1,9},{5,13},{9,1},{13,5},{2,10},{6,14},... | collective-permute-start | bytes 786440 | tf_op jit(solution)/shard_map/ppermute | solution.py:53
  66.0 11.4 %collective-permute-start.13 = (bf16[8,64,256]{2,1,0:T(8,128)(2,1)S(1)}, bf16[8,64,256]{2,1,0:T(8,128)(2,1)S(1)}, u32[]{:S(2)}, u32[]{:S(2)}) collective-permute-start(bf16[8,64,256]{2,1,0:T(8,128)(2,1)S(1)} %all-to-all-done.1.refs_8_), channel_id=1, source_target_pairs={{0,4},{4,8},{8,12},{12,0},{1,5},{5,9},{9,13},{13,1},{2,6},{6,10},{... | collective-permute-start | bytes 786440 | tf_op jit(solution)/shard_map/ppermute | solution.py:53
  70.9 16.9 %collective-permute-start.17 = (bf16[32,1024]{1,0:T(8,128)(2,1)S(1)}, bf16[32,1024]{1,0:T(8,128)(2,1)S(1)}, u32[]{:S(2)}, u32[]{:S(2)}) collective-permute-start(bf16[32,1024]{1,0:T(8,128)(2,1)S(1)} %get-tuple-element.54), channel_id=1, source_target_pairs={{0,3},{1,0},{2,1},{3,2},{4,7},{5,4},{6,5},{7,6},{8,11},{9,8},{10,9... | collective-permute-start | bytes 196616 | tf_op jit(solution)/shard_map/ppermute | solution.py:53
  74.9 12.9 %collective-permute-start.18 = (bf16[32,1024]{1,0:T(8,128)(2,1)S(1)}, bf16[32,1024]{1,0:T(8,128)(2,1)S(1)}, u32[]{:S(2)}, u32[]{:S(2)}) collective-permute-start(bf16[32,1024]{1,0:T(8,128)(2,1)S(1)} %get-tuple-element.55), channel_id=1, source_target_pairs={{0,2},{1,3},{2,0},{3,1},{4,6},{5,7},{6,4},{7,5},{8,10},{9,11},{10,... | collective-permute-start | bytes 196616 | tf_op jit(solution)/shard_map/ppermute | solution.py:53
  77.4 10.4 %collective-permute-start.19 = (bf16[32,1024]{1,0:T(8,128)(2,1)S(1)}, bf16[32,1024]{1,0:T(8,128)(2,1)S(1)}, u32[]{:S(2)}, u32[]{:S(2)}) collective-permute-start(bf16[32,1024]{1,0:T(8,128)(2,1)S(1)} %get-tuple-element.56), channel_id=1, source_target_pairs={{0,1},{1,2},{2,3},{3,0},{4,5},{5,6},{6,7},{7,4},{8,9},{9,10},{10,1... | collective-permute-start | bytes 196616 | tf_op jit(solution)/shard_map/ppermute | solution.py:53
  83.8 7.4 %collective-permute-start.16 = (f32[136,1024]{1,0:T(8,128)S(1)}, f32[136,1024]{1,0:T(8,128)S(1)}, u32[]{:S(2)}, u32[]{:S(2)}) collective-permute-start(f32[136,1024]{1,0:T(8,128)S(1)} %get-tuple-element.52), channel_id=1, source_target_pairs={{0,16},{16,0},{32,48},{48,32},{64,80},{80,64},{96,112},{112,96},{1... | collective-permute-start | bytes 1671176 | tf_op jit(solution)/shard_map/ppermute | solution.py:63
  87.8 3.4 %collective-permute-start.20 = (f32[128,1024]{1,0:T(8,128)S(1)}, f32[128,1024]{1,0:T(8,128)S(1)}, u32[]{:S(2)}, u32[]{:S(2)}) collective-permute-start(f32[128,1024]{1,0:T(8,128)S(1)} %get-tuple-element.57), channel_id=1, source_target_pairs={{0,16},{16,0},{32,48},{48,32},{64,80},{80,64},{96,112},{112,96},{1... | collective-permute-start | bytes 1572872 | tf_op jit(solution)/shard_map/ppermute | solution.py:63
  (5 other events, 13.7 us)
